TPU v7x, 32 devices: a whole 2x2x4 slice. The times are simulated.
32 devices in a mesh: dp: 16 (over z, x, core), tensor: 2 (over y).
Axes of the slice: x: 2, y: 2, z: 4, core: 2. Of those that a mesh axis runs over, the one named last changes fastest.
Arguments:
- tokens: bfloat16 [16384, 1024], P(('dp', 'tensor')), may hold values from -6 to 6
- cond: bfloat16 [16, 1024], P('dp'), may hold values from -6 to 6
- ada_w: bfloat16 [1024, 6, 1024], P('dp', None, 'tensor'), may hold values from -0.1875 to 0.1875
- ada_b: bfloat16 [6, 16, 64], P(None, 'tensor', 'dp'), may hold values from -3 to 3
- qkv_w: bfloat16 [1024, 3, 1024], P('dp', None, 'tensor'), may hold values from -0.1875 to 0.1875
- qv_b: bfloat16 [2, 16, 64], P(None, 'tensor', 'dp'), may hold values from -3 to 3
- proj_w: bfloat16 [1024, 1024], P('tensor', 'dp'), may hold values from -3 to 3
- proj_b: bfloat16 [1024], P('dp'), may hold values from -3 to 3
- fc1_w: bfloat16 [1024, 4096], P('dp', 'tensor'), may hold values from -0.1875 to 0.1875
- fc1_b: bfloat16 [64, 64], P('tensor', 'dp'), may hold values from -3 to 3
- fc2_w: bfloat16 [4096, 1024], P('tensor', 'dp'), may hold values from -0.09375 to 0.09375
- fc2_b: bfloat16 [1024], P('dp'), may hold values from -3 to 3
- grad_out: bfloat16 [16384, 1024], P(('dp', 'tensor')), may hold values from -6 to 6
Outputs:
- block_out: bfloat16 [16384, 1024], P(('dp', 'tensor'))
- grad_tokens: bfloat16 [16384, 1024], P(('dp', 'tensor'))
- grad_cond: bfloat16 [16, 1024], P('dp')
- grad_ada_w: float32 [1024, 6, 1024], P('dp', None, 'tensor')
- grad_ada_b: float32 [6, 16, 64], P(None, 'tensor', 'dp')
- grad_qkv_w: float32 [1024, 3, 1024], P('dp', None, 'tensor')
- grad_qv_b: float32 [2, 16, 64], P(None, 'tensor', 'dp')
- grad_proj_w: float32 [1024, 1024], P('tensor', 'dp')
- grad_proj_b: float32 [1024], P('dp')
- grad_fc1_w: float32 [1024, 4096], P('dp', 'tensor')
- grad_fc1_b: float32 [64, 64], P('tensor', 'dp')
- grad_fc2_w: float32 [4096, 1024], P('tensor', 'dp')
- grad_fc2_b: float32 [1024], P('dp')
All inputs are finite; a program needn't handle non-finite values.
Results may differ from a plain program's by a relative error of at most 0.02.
The roundings to bfloat16 on the way count: a program that leaves them out, or rounds other values in their place, can miss the bound.
Values may be sent and summed in bfloat16 or wider, within the bound.
No kernel may reach another device: no remote copies, remote signals or barrier semaphores. Data moves between devices by JAX's collectives and lax.ppermute only.
A program may use at most 256 MiB of HBM per device.

v0:
```python
import functools

import jax
import jax.numpy as jnp
from jax import lax
from jax.experimental import pallas as pl
from jax.experimental.pallas import tpu as pltpu
from jax.sharding import PartitionSpec as P

eps_norm = 1e-06
log2_e = 1.4426950408889634
both_axes = ("dp", "tensor")
f32 = jnp.float32
bf16 = jnp.bfloat16


def normalize(values):
    centre = values - jnp.mean(values, axis=-1, keepdims=True)
    inverse = lax.rsqrt(jnp.mean(centre * centre, axis=-1, keepdims=True) + eps_norm)
    return (centre * inverse, inverse)


def norm_back(grad_normed, normed, inverse):
    first = jnp.mean(grad_normed, axis=-1, keepdims=True)
    second = jnp.mean(grad_normed * normed, axis=-1, keepdims=True)
    return inverse * (grad_normed - first - normed * second)


def gelu_tanh(values):
    return jax.nn.gelu(values, approximate=True)


def dot_rows(left, right):
    return lax.dot_general(left, right, (((1,), (0,)), ((), ())), preferred_element_type=f32)


def dot_last(left, right):
    return lax.dot_general(left, right, (((1,), (1,)), ((), ())), preferred_element_type=f32)


def dot_first(left, right):
    return lax.dot_general(left, right, (((0,), (0,)), ((), ())), preferred_element_type=f32)


def head_masks(lanes, head_size):
    lane = lax.broadcasted_iota(jnp.int32, (1, lanes), 1)
    return [
        (lane >= h * head_size) & (lane < (h + 1) * head_size) for h in range(lanes // head_size)
    ]


def attend_kernel(head_size, q_ref, k_ref, v_ref, out_ref):
    lanes = q_ref.shape[1]
    masks = head_masks(lanes, head_size)
    factor = head_size**-0.5 * log2_e
    queries = q_ref[...]
    keys = k_ref[...]
    values = v_ref[...]
    result = None
    for mask in masks:
        scores = dot_last(jnp.where(mask, queries, jnp.zeros_like(queries)), keys)
        top = jnp.max(scores, axis=1, keepdims=True)
        powers = jnp.exp2((scores - top) * factor)
        total = jnp.sum(powers, axis=1, keepdims=True)
        part = dot_rows(powers.astype(bf16), values) * (1.0 / total)
        result = part if result is None else jnp.where(mask, part, result)
    out_ref[...] = result.astype(bf16)


def attend_back_kernel(head_size, q_ref, k_ref, v_ref, g_ref, *refs):
    out_ref, sum_k, sum_v = refs[-3:]
    lanes = q_ref.shape[1]
    masks = head_masks(lanes, head_size)
    scale = head_size**-0.5
    factor = scale * log2_e
    step = pl.program_id(1)

    @pl.when(step == 0)
    def _():
        queries = q_ref[...]
        grads = g_ref[...]
        keys = k_ref[...]
        values = v_ref[...]
        zero = jnp.zeros_like(keys)
        result = None
        for h, mask in enumerate(masks):
            scores = dot_last(jnp.where(mask, keys, zero), queries)
            top = jnp.max(scores, axis=0, keepdims=True)
            powers = jnp.exp2((scores - top) * factor)
            probs = powers * (1.0 / jnp.sum(powers, axis=0, keepdims=True))
            grad_probs = dot_last(jnp.where(mask, values, zero), grads)
            inner = jnp.sum(probs * grad_probs, axis=0, keepdims=True)
            grad_scores = (probs * (grad_probs - inner)).astype(bf16)
            sum_v[h] = dot_rows(probs.astype(bf16), grads)
            sum_k[h] = dot_rows(grad_scores, queries)
            part = dot_first(grad_scores, keys)
            result = part if result is None else jnp.where(mask, part, result)
        out_ref[...] = (result * scale).astype(bf16)

    def joined(sums):
        total = sums[0]
        for h in range(1, len(masks)):
            total = jnp.where(masks[h], sums[h], total)
        return total

    @pl.when(step == 1)
    def _():
        out_ref[...] = (joined(sum_k) * scale).astype(bf16)

    @pl.when(step == 2)
    def _():
        out_ref[...] = joined(sum_v).astype(bf16)


def column_spec(rows, lanes, first, row_block=0):
    return pl.BlockSpec((rows, lanes), lambda j: (row_block, first + j))


def attention(projected, row_block, row_blocks, part_width, head_size):
    rows = projected.shape[0]
    here = rows // row_blocks
    lanes = min(128, part_width)
    count = part_width // lanes
    work = rows * here * part_width
    return pl.pallas_call(
        functools.partial(attend_kernel, head_size),
        out_shape=jax.ShapeDtypeStruct((here, part_width), bf16),
        grid=(count,),
        in_specs=[
            column_spec(here, lanes, 0, row_block),
            column_spec(rows, lanes, count),
            column_spec(rows, lanes, 2 * count),
        ],
        out_specs=column_spec(here, lanes, 0),
        compiler_params=pltpu.CompilerParams(vmem_limit_bytes=40 * 1024 * 1024),
        cost_estimate=pl.CostEstimate(
            flops=16 * work,
            bytes_accessed=8 * rows * part_width,
            transcendentals=work // head_size,
        ),
    )(projected, projected, projected)


def attention_back(projected, grads, earlier, first, blocks, part_width, head_size):
    rows = projected.shape[0]
    lanes = min(128, part_width)
    count = part_width // lanes
    work = rows * rows * blocks * lanes
    sums = pltpu.VMEM((lanes // head_size, rows, lanes), f32)

    def items(part):
        return pl.BlockSpec((rows, lanes), lambda j, p: (0, part * count + first + j))

    in_specs = [items(0), items(1), items(2), items(0)]
    operands = [projected, projected, projected, grads]
    aliases = {}
    if earlier is not None:
        in_specs.append(pl.BlockSpec(memory_space=pl.ANY))
        operands.append(earlier)
        aliases = {4: 0}
    return pl.pallas_call(
        functools.partial(attend_back_kernel, head_size),
        out_shape=jax.ShapeDtypeStruct((rows, 3 * part_width), bf16),
        grid=(blocks, 3),
        in_specs=in_specs,
        out_specs=pl.BlockSpec((rows, lanes), lambda j, p: (0, p * count + first + j)),
        scratch_shapes=[sums, sums],
        input_output_aliases=aliases,
        compiler_params=pltpu.CompilerParams(vmem_limit_bytes=48 * 1024 * 1024),
        cost_estimate=pl.CostEstimate(
            flops=40 * work,
            bytes_accessed=14 * rows * blocks * lanes,
            transcendentals=work // head_size,
        ),
    )(*operands)


def add_sums(sum_ref, terms):
    @pl.when(pl.program_id(0) == 0)
    def _():
        sum_ref[...] = jnp.zeros_like(sum_ref)

    for number, term in enumerate(terms):
        sum_ref[number : number + 1, :] += jnp.sum(term, axis=0, keepdims=True)


def middle_kernel(tokens_ref, branch_ref, bias_ref, mod_ref, resid_ref, low_ref):
    resid = tokens_ref[...].astype(f32) + mod_ref[2:3, :] * (branch_ref[...] + bias_ref[...])
    resid_ref[...] = resid
    normed, _ = normalize(resid)
    low_ref[...] = (normed * (1.0 + mod_ref[4:5, :]) + mod_ref[3:4, :]).astype(bf16)


def middle_back_kernel(
    resid_ref, branch_ref, own_ref, other_ref, top_ref, bias_ref, mod_ref, grad_ref, low_ref, sum_ref
):
    grad_in = own_ref[...] + other_ref[...].astype(f32)
    normed, inverse = normalize(resid_ref[...])
    back = norm_back(grad_in * (1.0 + mod_ref[4:5, :]), normed, inverse)
    grads = top_ref[...].astype(f32) + back
    grad_ref[...] = grads
    low = (mod_ref[2:3, :] * grads).astype(bf16)
    low_ref[...] = low
    branch = branch_ref[...] + bias_ref[...]
    add_sums(sum_ref, (grads * branch, grad_in, grad_in * normed, low.astype(f32)))


def first_back_kernel(tokens_ref, own_ref, other_ref, grad_ref, mod_ref, out_ref, sum_ref):
    grad_in = own_ref[...] + other_ref[...].astype(f32)
    normed, inverse = normalize(tokens_ref[...].astype(f32))
    back = norm_back(grad_in * (1.0 + mod_ref[1:2, :]), normed, inverse)
    out_ref[...] = (grad_ref[...] + back).astype(bf16)
    add_sums(sum_ref, (grad_in, grad_in * normed))


def finish_kernel(resid_ref, own_ref, other_ref, top_ref, bias_ref, mod_ref, out_ref, sum_ref):
    branch = own_ref[...] + other_ref[...].astype(f32) + bias_ref[...]
    out_ref[...] = (resid_ref[...] + mod_ref[5:6, :] * branch).astype(bf16)
    add_sums(sum_ref, (top_ref[...].astype(f32) * branch,))


def over_rows(kernel, many, single, kinds, summed):
    rows, width = many[0].shape
    block = min(128, rows)
    spec = pl.BlockSpec((block, width), lambda i: (i, 0))
    in_specs = [spec] * len(many)
    in_specs += [pl.BlockSpec(v.shape, lambda i: (0, 0)) for v in single]
    out_specs = [spec] * len(kinds)
    out_shape = [jax.ShapeDtypeStruct((rows, width), kind) for kind in kinds]
    if summed:
        out_specs.append(pl.BlockSpec((8, width), lambda i: (0, 0)))
        out_shape.append(jax.ShapeDtypeStruct((8, width), f32))
    return pl.pallas_call(
        kernel,
        out_shape=out_shape,
        grid=(rows // block,),
        in_specs=in_specs,
        out_specs=out_specs,
        compiler_params=pltpu.CompilerParams(vmem_limit_bytes=32 * 1024 * 1024),
        cost_estimate=pl.CostEstimate(
            flops=20 * rows * width, bytes_accessed=16 * rows * width, transcendentals=0
        ),
    )(*many, *single)


class PairPlan:
    def __init__(self, dp_size):
        self.dp_size = dp_size
        self.index = lax.axis_index("dp")
        self.masks = [1 << b for b in range(dp_size.bit_length() - 1)]
        self.blocks = 2

    def tie(self, values, *others):
        return lax.optimization_barrier((values,) + others)[0]

    def across(self, values):
        return lax.ppermute(values, "tensor", [(0, 1), (1, 0)])

    def swap(self, values, mask):
        return lax.ppermute(values, "dp", [(i, i ^ mask) for i in range(self.dp_size)])

    def upper(self, mask):
        return (self.index // mask) % 2 == 1

    def join(self, own, other, upper, axis):
        return jnp.stack([jnp.where(upper, other, own), jnp.where(upper, own, other)], axis=axis)

    def gather_dp(self, values):
        gathered = values
        for low in self.masks[::2]:
            items = [gathered] + [self.swap(gathered, low * other) for other in (1, 2, 3)]
            place = (self.index // low) % 4
            gathered = jnp.stack([self.choose(items, place ^ slot) for slot in range(4)])
        return gathered.reshape((-1,) + values.shape)

    def choose(self, items, which):
        chosen = items[3]
        for number in range(3):
            chosen = jnp.where(which == number, items[number], chosen)
        return chosen

    def reduce_small(self, values):
        shape = values.shape[1:]
        for low in self.masks[::2][::-1]:
            values = values.reshape((4, -1) + shape)
            place = (self.index // low) % 4
            items = [values[slot] for slot in range(4)]
            total = self.choose(items, place)
            for other in (1, 2, 3):
                total = total + self.swap(self.choose(items, place ^ other), low * other)
            values = total
        return values[0]

    def step(self, values, mask, axis):
        upper = self.upper(mask)
        low = lax.index_in_dim(values, 0, axis, keepdims=False)
        high = lax.index_in_dim(values, 1, axis, keepdims=False)
        return jnp.where(upper, high, low), self.swap(jnp.where(upper, low, high), mask)

    def add(self, own, received):
        return (own.astype(f32) + received.astype(f32)).astype(bf16)

    def hold(self, *values):
        return lax.optimization_barrier(values)

    def send(self, rows):
        return self.across(rows)

    def gather(self, rows, received):
        return [rows, received]

    def scatter(self, term):
        sent = term(1, None).astype(bf16)
        received = self.across(sent)
        return term(0, sent), received

    def pair(self, own, received):
        return own, received

    def columns(self, values):
        other = self.across(values)
        second = lax.axis_index("tensor") == 1
        return jnp.concatenate(
            [jnp.where(second, other, values), jnp.where(second, values, other)], axis=1
        )

    def scatter_columns(self, values):
        half = values.shape[1] // 2
        second = lax.axis_index("tensor") == 1
        low = values[:, :half]
        high = values[:, half:]
        return jnp.where(second, high, low) + self.across(jnp.where(second, low, high))

    def sum_tensor(self, values):
        return values + self.across(values)


class AxisPlan:
    def __init__(self):
        self.blocks = 1

    def tie(self, values, *others):
        return values

    def gather_dp(self, values):
        return lax.all_gather(values, "dp", axis=0)

    def reduce_small(self, values):
        return lax.psum_scatter(values, "dp", scatter_dimension=0, tiled=False)

    def hold(self, *values):
        return values

    def scatter_last(self, grads):
        return lax.psum_scatter(grads, "dp", scatter_dimension=0, tiled=True)

    def send(self, rows):
        return rows

    def gather(self, rows, received):
        return [lax.all_gather(rows, "tensor", axis=0, tiled=True)]

    def scatter(self, term):
        return (
            lax.psum_scatter(term(0, None).astype(bf16), "tensor", scatter_dimension=0, tiled=True),
            None,
        )

    def pair(self, own, received):
        return own.astype(f32), jnp.zeros(own.shape, bf16)

    def columns(self, values):
        return lax.all_gather(values, "tensor", axis=1, tiled=True)

    def scatter_columns(self, values):
        return lax.psum_scatter(values, "tensor", scatter_dimension=1, tiled=True)

    def sum_tensor(self, values):
        return lax.psum(values, "tensor")


def stack_rows(blocks):
    return blocks[0] if len(blocks) == 1 else jnp.concatenate(blocks, axis=0)


def body(
    dp_size,
    parts,
    tokens,
    cond,
    ada_w,
    ada_b,
    qkv_w,
    qv_b,
    proj_w,
    proj_b,
    fc1_w,
    fc1_b,
    fc2_w,
    fc2_b,
    grad_out,
):
    paired = parts == 2 and dp_size in (4, 16, 64)
    plan = PairPlan(dp_size) if paired else AxisPlan()
    dp_index = lax.axis_index("dp")
    width = tokens.shape[1]
    shard = ada_w.shape[0]
    part_width = qkv_w.shape[2]
    hidden_part = fc1_w.shape[1]
    heads_part = qv_b.shape[1]
    piece = qv_b.shape[2]
    head_size = piece * dp_size
    qkv_width = 3 * part_width
    extra = 128
    assert cond.shape[0] == 1

    proj_shard = proj_w.T
    if paired:
        proj_shard = jnp.concatenate([proj_shard, plan.send(proj_shard)], axis=1)
    first_shard = jnp.concatenate([qkv_w.reshape(shard, qkv_width), proj_shard], axis=1)

    def gather_weight(values):
        return lax.all_gather(values, "dp", axis=0, tiled=True)

    def scatter_weight(values):
        return lax.psum_scatter(values, "dp", scatter_dimension=1, tiled=True)

    first_full = gather_weight(first_shard)
    tokens_all = plan.gather(tokens, plan.send(tokens))
    grad_out_sent = plan.send(plan.tie(grad_out, tokens_all[-1]))

    small = plan.gather_dp(
        jnp.concatenate([v.reshape(-1) for v in (cond, proj_b, fc2_b, ada_b, qv_b, fc1_b)])
    )
    mlp_shard = jnp.stack([fc1_w, fc2_w.T])
    mlp_full = lax.all_gather(plan.tie(mlp_shard, small), "dp", axis=1, tiled=True)
    fc1_full = mlp_full[0]
    fc2_full = mlp_full[1]
    start = width + 2 * shard
    cond_all = small[:, :width].astype(f32)
    proj_bias = small[:, width : width + shard].reshape(width).astype(f32)
    fc2_bias = small[:, width + shard : start].reshape(width).astype(f32)
    head_bias = small[:, start:].reshape(dp_size, -1, piece).transpose(1, 0, 2).reshape(-1)
    head_bias = plan.hold(head_bias)[0].astype(f32)
    ada_bias = head_bias[: 6 * part_width].reshape(6, part_width)
    qv_bias = head_bias[6 * part_width : 8 * part_width].reshape(2, part_width)
    fc1_bias = head_bias[8 * part_width :]
    silu_all = jax.nn.silu(cond_all).astype(bf16)
    silu_own = lax.dynamic_slice_in_dim(silu_all, dp_index * shard, shard, axis=1)
    mod_terms = jnp.einsum("ld,dke->lke", silu_own, ada_w, preferred_element_type=f32)
    mod_part = plan.tie(plan.reduce_small(mod_terms) + ada_bias, tokens_all[-1])
    modulation = plan.columns(mod_part)
    shift_one, scale_one, gate_two = [modulation[k : k + 1] for k in (0, 1, 5)]

    attn_blocks = []
    for rows in tokens_all:
        normed, _ = normalize(rows.astype(f32))
        attn_blocks.append((normed * (1.0 + scale_one) + shift_one).astype(bf16))
    qkv_full = first_full[:, :qkv_width]
    qkv_bias = jnp.concatenate([qv_bias[0], jnp.zeros((part_width,), f32), qv_bias[1]])
    attn_all = stack_rows(attn_blocks)
    projected = (dot_rows(attn_all, qkv_full) + qkv_bias).astype(bf16)

    proj_full = first_full[:, qkv_width : qkv_width + part_width]
    far_proj = first_full[:, qkv_width + part_width :]
    grad_two = [
        (gate_two * rows.astype(f32)).astype(bf16) for rows in plan.gather(grad_out, grad_out_sent)
    ]
    grad_two_all = stack_rows(grad_two)
    attended = [None] * plan.blocks

    def rows_of(values, block):
        count = values.shape[0] // plan.blocks
        return values[block * count : (block + 1) * count]

    def attend(block, items):
        return attention(items, block, plan.blocks, part_width, head_size)

    def attend_term(block, earlier):
        attended[block] = attend(block, projected)
        return dot_last(attended[block], proj_full)

    if paired:
        attended_sent = plan.send(attend(1, projected))
        attended_own = attend(0, plan.tie(projected, grad_out_sent))
        branch_one = dot_last(attended_own, proj_full) + dot_last(attended_sent, far_proj)
    else:
        branch_one = plan.scatter(attend_term)[0].astype(f32)
    proj_bias = proj_bias.reshape(1, width)
    fc2_bias = fc2_bias.reshape(1, width)
    residual_mid, mlp_low = over_rows(
        middle_kernel, (tokens, branch_one), (proj_bias, modulation), (f32, bf16), False
    )
    mlp_blocks = plan.gather(mlp_low, plan.send(mlp_low))
    mlp_all = stack_rows(mlp_blocks)
    active_blocks = [None] * plan.blocks

    grad_hidden = [None] * plan.blocks

    def mlp_back_term(block, earlier):
        grads, rows = grad_two[block], mlp_blocks[block]
        if earlier is not None:
            grads, rows, _ = plan.hold(grads, rows, earlier)
        hidden = dot_rows(rows, fc1_full) + fc1_bias
        activated, pull = jax.vjp(gelu_tanh, hidden)
        active_blocks[block] = activated.astype(bf16)
        grad_hidden[block] = pull(dot_rows(grads, fc2_full))[0].astype(bf16)
        return dot_last(grad_hidden[block], fc1_full)

    grad_mlp_own, grad_mlp_sent = plan.scatter(mlp_back_term)
    grad_hidden_all = stack_rows(grad_hidden)
    active = stack_rows(active_blocks)
    mlp_sums = lax.dot_general(
        jnp.stack([mlp_all, grad_two_all]),
        jnp.stack([grad_hidden_all, active]),
        (((1,), (1,)), ((0,), (0,))),
        preferred_element_type=f32,
    ).astype(bf16)
    second_sum = lax.psum_scatter(mlp_sums, "dp", scatter_dimension=1, tiled=True)
    grad_mlp_own = plan.tie(grad_mlp_own, mlp_sums)
    grad_resid, grad_branch_one, middle_sums = over_rows(
        middle_back_kernel,
        (residual_mid, branch_one, *plan.pair(grad_mlp_own, grad_mlp_sent), grad_out),
        (proj_bias, modulation),
        (f32, bf16),
        True,
    )
    proj_sum = middle_sums[3]
    grad_proj_sent = None
    if paired:
        far_grads = dot_rows(grad_branch_one, far_proj).astype(bf16)
        grad_attended_sent = plan.send(far_grads)
        grad_attended = dot_rows(grad_branch_one, proj_full).astype(bf16)
        grad_rows = plan.tie(grad_branch_one, far_grads)
        far_proj_sum = dot_first(grad_rows, attended_sent).astype(bf16)
        grad_proj = dot_first(grad_rows, attended_own).astype(bf16)
        grad_attended_sent = plan.tie(grad_attended_sent, far_proj_sum, grad_proj)
        grad_proj_sent = plan.send(plan.tie(far_proj_sum, grad_attended_sent))
        proj_sum = plan.sum_tensor(plan.tie(proj_sum, grad_attended_sent))
        grad_attended = stack_rows([grad_attended, grad_attended_sent])
    else:
        grad_one_all = stack_rows(plan.gather(grad_branch_one, plan.send(grad_branch_one)))
        proj_sum = jnp.sum(grad_one_all, axis=0, dtype=f32)
        grad_proj = dot_first(grad_one_all, stack_rows(attended)).astype(bf16)
        grad_attended = dot_rows(grad_one_all, proj_full).astype(bf16)

    if paired:
        far_rows = dot_last(plan.tie(active_blocks[1], far_grads), fc2_full).astype(bf16)
    else:
        branch_two = plan.scatter(lambda block, e: dot_last(active_blocks[0], fc2_full))[0]
        branch_two_parts = plan.pair(branch_two, None)

    def token_sum(values):
        return jnp.sum(values, axis=0, dtype=f32)

    head_sums = token_sum(grad_hidden_all)
    head_sums = head_sums.reshape(-1, dp_size, piece).transpose(1, 0, 2).reshape(dp_size, -1)
    bias_sums = jnp.concatenate(
        [
            head_sums,
            proj_sum.reshape(dp_size, shard),
            token_sum(grad_two_all).reshape(dp_size, shard),
        ],
        axis=1,
    ).astype(bf16)
    bias_sums = jnp.pad(bias_sums, ((0, 0), (0, shard * extra - bias_sums.shape[1])))
    bias_sums = bias_sums.reshape(width, extra)
    lane_blocks = part_width // min(128, part_width)
    calls = 2 if lane_blocks % 2 == 0 else 1
    grad_projected = None
    for call in range(calls):
        if call == 1 and paired:
            grad_attended, grad_proj_sent, bias_sums, grad_projected, far_rows = plan.hold(
                grad_attended, grad_proj_sent, bias_sums, grad_projected, far_rows
            )
            branch_two_sent = plan.send(far_rows)
        grad_projected = attention_back(
            projected,
            grad_attended,
            grad_projected,
            call * (lane_blocks // calls),
            lane_blocks // calls,
            part_width,
            head_size,
        )

    def attn_back_term(block, earlier):
        items = rows_of(grad_projected, block)
        if earlier is not None:
            items = plan.tie(items, earlier)
        return dot_last(items, qkv_full)

    if paired:
        branch_two_sent, grad_projected = plan.hold(branch_two_sent, grad_projected)
    grad_attn_own, grad_attn_sent = plan.scatter(attn_back_term)
    if paired:
        own_active, grad_attn_own = plan.hold(active_blocks[0], grad_attn_own)
        branch_two_parts = (dot_last(own_active, fc2_full), branch_two_sent)
    block_out, last_sums = over_rows(
        finish_kernel,
        (residual_mid, *branch_two_parts, grad_out),
        (fc2_bias, modulation),
        (bf16,),
        True,
    )
    grad_attn_own, grad_projected, block_out, last_sums = plan.hold(
        grad_attn_own, grad_projected, block_out, last_sums
    )
    qkv_sums = token_sum(grad_projected)
    qv_sums = jnp.stack([qkv_sums[:part_width], qkv_sums[2 * part_width :]]).astype(bf16)
    first_sum = dot_first(attn_all, grad_projected).astype(bf16)
    if paired:
        grad_proj = plan.add(grad_proj, grad_proj_sent)
    first_sum = jnp.concatenate([first_sum, grad_proj, bias_sums], axis=1)
    if paired:
        first_sum = first_sum.reshape((2, 2, 2, 2, shard, -1))
        half = first_sum.shape[-1] // 256 * 128
        first_sum, grad_attn_sent, qv_sums = plan.hold(first_sum, grad_attn_sent, qv_sums)
        held, received = plan.step(first_sum, 1, 3)
        first_sum = plan.add(held, received)
        one = plan.step(first_sum[..., :half], 2, 2)
        two = plan.step(first_sum[..., half:], 4, 1)
    else:
        first_sum = plan.scatter_last(first_sum)
    grad_tokens, first_sums = over_rows(
        first_back_kernel,
        (tokens, *plan.pair(grad_attn_own, grad_attn_sent), grad_resid),
        (modulation,),
        (bf16,),
        True,
    )
    sums = jnp.concatenate([first_sums[:2], middle_sums[:3], last_sums[:1]], axis=0)
    grad_mod = plan.scatter_columns(sums).astype(bf16)
    grad_mod, second_sum = plan.hold(grad_mod, second_sum)
    grad_mod = plan.gather_dp(jnp.concatenate([grad_mod, qv_sums], axis=0))
    qv_sums = jnp.sum(grad_mod[:, 6:], axis=0, dtype=f32).reshape(2, heads_part, head_size)
    grad_qv_b = lax.dynamic_slice_in_dim(qv_sums, dp_index * piece, piece, axis=2)
    grad_mod = grad_mod[:, :6]
    if paired:
        one_sent, two_sent, grad_mod = plan.hold(one[1], two[1], grad_mod)
        one = plan.step(plan.add(one[0], one_sent), 4, 1)
        two = plan.step(plan.add(two[0], two_sent), 8, 0)
    grad_silu = jnp.einsum("lke,dke->ld", grad_mod, ada_w, preferred_element_type=f32)
    grad_silu = plan.sum_tensor(grad_silu)
    if paired:
        one_sent, two_sent, grad_silu = plan.hold(one[1], two[1], grad_silu)
        one = plan.step(plan.add(one[0], one_sent), 8, 0)
        two = plan.step(plan.add(two[0], two_sent), 2, 0)
    grad_silu = plan.gather_dp(grad_silu)
    if paired:
        first_sum = jnp.concatenate([plan.add(*one), plan.add(*two)], axis=-1)
    grad_ada_w = jnp.einsum("ld,lke->dke", silu_own, grad_mod, preferred_element_type=f32)
    grad_ada_b = jnp.sum(grad_mod, axis=0, dtype=f32).reshape(6, heads_part, head_size)
    grad_ada_b = lax.dynamic_slice_in_dim(grad_ada_b, dp_index * piece, piece, axis=2)
    grad_silu = lax.dynamic_index_in_dim(grad_silu, dp_index, 1, keepdims=False).reshape(1, width)
    grad_cond = jax.vjp(jax.nn.silu, cond.astype(f32))[1](grad_silu)[0].astype(bf16)

    owned = first_sum[:, qkv_width + part_width :].reshape(-1).astype(f32)
    start = fc1_b.size
    grad_fc1_b = owned[:start].reshape(fc1_b.shape)
    return (
        block_out,
        grad_tokens,
        grad_cond,
        grad_ada_w,
        grad_ada_b,
        first_sum[:, :qkv_width].astype(f32).reshape(qkv_w.shape),
        grad_qv_b,
        first_sum[:, qkv_width : qkv_width + part_width].astype(f32).T,
        owned[start : start + shard],
        second_sum[0].astype(f32),
        grad_fc1_b,
        second_sum[1].astype(f32).T,
        owned[start + shard : start + 2 * shard],
    )


def solution(mesh):
    rows = P(("dp", "tensor"), None)
    ada = P("dp", None, "tensor")
    heads = P(None, "tensor", "dp")
    out = P("tensor", "dp")
    weights = (ada, heads, ada, heads, out, P("dp"), P("dp", "tensor"), out, out, P("dp"))
    return jax.shard_map(
        functools.partial(body, mesh.shape["dp"], mesh.shape["tensor"]),
        mesh=mesh,
        in_specs=(rows, P("dp", None)) + weights + (rows,),
        out_specs=(rows, rows, P("dp", None)) + weights,
        check_vma=False,
    )
```

profile of v0, /device:TPU:0, one launch (start us, length us, event | category | flops | bytes accessed | tf_op | source)
XLA Modules:
  0.0 383.4 jit_solution(3749051946427371023)
XLA Ops:
  7.3 3.0 collective-permute-start.14
  25.1 3.7 collective-permute-start.5
  50.3 3.1 collective-permute-done.7
  69.7 3.7 all-gather.3.cloned.1.call-done
  73.4 5.9 %add_convert_fusion.q_ref.k_ref.v_ref = bf16[1024,1536]{1,0:T(8,128)(2,1)S(1)} fusion(f32[1536]{0:T(1024)} %pad_maximum_fusion.16, bf16[1024,2560]{1,0:T(8,128)(2,1)} %all-gather.3.cloned.1.call-done, bf16[512,1024]{1,0:T(8,128)(2,1)} %get-tuple-element.210, bf16[512,1024]{1,0:T(8,128)(2,1)} %get-tuple-element.209), kind=kOutput, calls=%fused_computation.4 | convolution fusion | flops 3228565504 | bytes 8396800 | tf_op jit(solution)/shard_map/dot_general | solution.py:34
  79.4 8.8 %shard_map.229 = bf16[512,512]{1,0:T(8,128)(2,1)S(1)} custom-call(bf16[1024,1536]{1,0:T(8,128)(2,1)S(1)} %add_convert_fusion.q_ref.k_ref.v_ref, bf16[1024,1536]{1,0:T(8,128)(2,1)S(1)} %add_convert_fusion.q_ref.k_ref.v_ref, bf16[1024,1536]{1,0:T(8,128)(2,1)S(1)} %add_convert_fusion.q_ref.k_ref.v_ref), custom_call_target="tpu_custom_call" | custom-call | flops 4294967296 | bytes 4194304 | tf_op jit(solution)/shard_map/pallas_call | solution.py:125
  94.7 8.6 %shard_map.228 = bf16[512,512]{1,0:T(8,128)(2,1)S(1)} custom-call(bf16[1024,1536]{1,0:T(8,128)(2,1)S(1)} %copy-done.23, bf16[1024,1536]{1,0:T(8,128)(2,1)S(1)} %copy-done.23, bf16[1024,1536]{1,0:T(8,128)(2,1)S(1)} %copy-done.23), custom_call_target="tpu_custom_call" | custom-call | flops 4294967296 | bytes 4194304 | tf_op jit(solution)/shard_map/pallas_call | solution.py:125
  113.6 3.4 fusion.98
  117.1 3.0 maximum_bitcast_fusion.3
  120.2 16.8 %collective-permute-done.17 = bf16[512,1024]{1,0:T(8,128)(2,1)} collective-permute-done((bf16[512,1024]{1,0:T(8,128)(2,1)}, bf16[512,1024]{1,0:T(8,128)(2,1)}, u32[]{:S(2)}, u32[]{:S(2)}) %collective-permute-start.17) | collective-permute-done | bytes 1048608 | tf_op jit(solution)/shard_map/ppermute | solution.py:257
  140.0 9.8 %all-gather.5.cloned.1.call-done = bf16[2,1024,2048]{2,1,0:T(8,128)(2,1)} async-done(((bf16[2,64,2048]{2,1,0:T(8,128)(2,1)}), bf16[2,1024,2048]{2,1,0:T(8,128)(2,1)}) %all-gather.5.cloned.1.call-update) | async-done | bytes 8388624 | tf_op jit(solution)/shard_map/all_gather | solution.py:436
  149.8 5.0 %fusion.32 = f32[512,2048]{1,0:T(8,128)S(1)} fusion(bf16[512,1024]{1,0:T(8,128)(2,1)} %collective-permute-done.17, bf16[2,1024,2048]{2,1,0:T(8,128)(2,1)} %all-gather.5.cloned.1.call-done), kind=kOutput, calls=%fused_computation.44 | convolution fusion | flops 2147483648 | bytes 9437184 | tf_op jit(solution)/shard_map/dot_general | solution.py:34
  155.0 5.8 %fusion.105 = (bf16[2048]{0:T(1024)(128)(2,1)}, bf16[512,2048]{1,0:T(8,128)(2,1)S(1)}) fusion(f32[512,2048]{1,0:T(8,128)S(1)} %fusion.32, f32[2048]{0:T(1024)S(1)} %copy-done.50, bf16[512,1024]{1,0:T(8,128)(2,1)S(1)} %copy-done.28, bf16[2,1024,2048]{2,1,0:T(8,128)(2,1)S(1)} %copy-done.51), kind=kOutput, calls=%fused_computation.231 | convolution fusion | flops 2170550272 | bytes 11546624 | tf_op jit(solution)/shard_map/dot_general | solution.py:34
  160.8 3.5 fusion.56
  165.7 5.9 %multiply_convert_fusion = (bf16[512,2048]{1,0:T(8,128)(2,1)S(1)}, bf16[512,2048]{1,0:T(8,128)(2,1)S(1)}, f32[512,2048]{1,0:T(8,128)S(1)}) fusion(f32[512,2048]{1,0:T(8,128)S(1)} %fusion.32, f32[2048]{0:T(1024)S(1)} %copy-done.50, bf16[512,1024]{1,0:T(8,128)(2,1)} %get-tuple-element.64, bf16[2,1024,2048]{2,1,0:T(8,128)(2,1)S(1)} %copy-done.51), kind=kOutput, calls=%fused_computation.34 | convolution fusion | flops 2168455168 | bytes 17833984 | tf_op jit(solution)/shard_map/dot_general | solution.py:34
  171.7 5.6 %fusion.104 = (bf16[2048]{0:T(1024)(128)(2,1)}, bf16[512,2048]{1,0:T(8,128)(2,1)S(1)}) fusion(f32[512,2048]{1,0:T(8,128)S(1)} %get-tuple-element.215, f32[2048]{0:T(1024)S(1)} %copy-done.50, bf16[512,1024]{1,0:T(8,128)(2,1)S(1)} %copy-done.27, bf16[2,1024,2048]{2,1,0:T(8,128)(2,1)S(1)} %copy-done.51), kind=kOutput, calls=%fused_computation.230 | convolution fusion | flops 2170550272 | bytes 11546624 | tf_op jit(solution)/shard_map/dot_general | solution.py:34
  180.2 13.1 %fusion.4 = bf16[2,1024,2048]{2,1,0:T(8,128)(2,1)} fusion(bf16[1,1024,2048]{2,1,0:T(8,128)(2,1)S(1)} %maximum_bitcast_fusion.1, bf16[1,1024,2048]{2,1,0:T(8,128)(2,1)S(1)} %maximum_bitcast_fusion, bf16[1,1024,1024]{2,1,0:T(8,128)(2,1)S(1)} %copy-done.29, bf16[1,1024,1024]{2,1,0:T(8,128)(2,1)} %maximum_bitcast_fusion.2), kind=kOutput, calls=%fused_computation.9 | convolution fusion | flops 8600420352 | bytes 20971520 | tf_op jit(solution)/shard_map/dot_general | solution.py:513
  197.7 5.4 %fusion.29.own_ref = f32[512,1024]{1,0:T(8,128)S(1)} fusion(bf16[512,2048]{1,0:T(8,128)(2,1)} %copy-done.34, bf16[2,1024,2048]{2,1,0:T(8,128)(2,1)} %all-gather.5.cloned.1.call-done), kind=kOutput, calls=%fused_computation.41 | convolution fusion | flops 2147483648 | bytes 8388608 | tf_op jit(solution)/shard_map/dot_general | solution.py:38
  203.1 4.4 %shard_map.231 = (f32[512,1024]{1,0:T(8,128)S(1)}, bf16[512,1024]{1,0:T(8,128)(2,1)S(1)}, f32[8,1024]{1,0:T(8,128)S(1)}) custom-call(f32[512,1024]{1,0:T(8,128)S(1)} %copy-done.6, f32[512,1024]{1,0:T(8,128)S(1)} %convolution_add_fusion.branch_ref, f32[512,1024]{1,0:T(8,128)S(1)} %fusion.29.own_ref, bf16[512,1024]{1,0:T(8,128)(2,1)} %collective-permute-done.18.other_ref, ...), custom_call_target="tpu_custom_call" | custom-call | flops 10485760 | bytes 8388608 | tf_op jit(solution)/shard_map/pallas_call | solution.py:233
  216.6 3.4 fusion.57
  219.9 4.3 %collective-permute-done.19 = bf16[512,512]{1,0:T(8,128)(2,1)S(1)} collective-permute-done((bf16[512,512]{1,0:T(8,128)(2,1)S(1)}, bf16[512,512]{1,0:T(8,128)(2,1)S(1)}, u32[]{:S(2)}, u32[]{:S(2)}) %collective-permute-start.19) | collective-permute-done | bytes 524320 | tf_op jit(solution)/shard_map/ppermute | solution.py:257
  226.3 18.3 %shard_map.232.refs_0_ = bf16[1024,1536]{1,0:T(8,128)(2,1)S(1)} custom-call(bf16[1024,1536]{1,0:T(8,128)(2,1)} %copy-done.22, bf16[1024,1536]{1,0:T(8,128)(2,1)} %copy-done.22, bf16[1024,1536]{1,0:T(8,128)(2,1)} %copy-done.22, bf16[1024,512]{1,0:T(8,128)(2,1)S(1)} %pad_maximum_fusion.4.g_ref), custom_call_target="tpu_custom_call" | custom-call | flops 10737418240 | bytes 3670016 | tf_op jit(solution)/shard_map/pallas_call | solution.py:161
  255.0 17.8 %shard_map.233 = bf16[1024,1536]{1,0:T(8,128)(2,1)S(1)} custom-call(bf16[1024,1536]{1,0:T(8,128)(2,1)} %copy-done.22, bf16[1024,1536]{1,0:T(8,128)(2,1)} %copy-done.22, bf16[1024,1536]{1,0:T(8,128)(2,1)} %copy-done.22, bf16[1024,512]{1,0:T(8,128)(2,1)S(1)} %pad_maximum_fusion.4.g_ref, bf16[1024,1536]{1,0:T(8,128)(2,1)S(1)} %copy-done.9), custom_call_target="tpu_custom_call", output_to_operand_aliasing={{}: (4, {})} | custom-call | flops 10737418240 | bytes 3670016 | tf_op jit(solution)/shard_map/pallas_call | solution.py:161
  273.7 4.9 %fusion.51 = bf16[512,1024]{1,0:T(8,128)(2,1)} fusion(bf16[1024,2560]{1,0:T(8,128)(2,1)} %all-gather.3.cloned.1.call-done, bf16[1024,1536]{1,0:T(8,128)(2,1)S(1)} %shard_map.233), kind=kOutput, calls=%fused_computation.75 | convolution fusion | flops 1611137024 | bytes 5767168 | tf_op jit(solution)/shard_map/dot_general | solution.py:38
  280.3 4.2 %fusion.37.own_ref = f32[512,1024]{1,0:T(8,128)S(1)} fusion(bf16[512,1536]{1,0:T(8,128)(2,1)S(1)} %slice.238, bf16[1024,2560]{1,0:T(8,128)(2,1)} %all-gather.3.cloned.1.call-done), kind=kOutput, calls=%fused_computation.53 | convolution fusion | flops 1610612736 | bytes 6815744 | tf_op jit(solution)/shard_map/dot_general | solution.py:38
  292.2 6.2 %convolution_convert_fusion = bf16[1024,1536]{1,0:T(8,128)(2,1)S(1)} fusion(bf16[1024,1536]{1,0:T(8,128)(2,1)} %copy-done.10, bf16[512,1024]{1,0:T(8,128)(2,1)} %get-tuple-element.210, bf16[512,1024]{1,0:T(8,128)(2,1)} %get-tuple-element.209), kind=kOutput, calls=%fused_computation.36 | convolution fusion | flops 3226992640 | bytes 8388608 | tf_op jit(solution)/shard_map/dot_general | solution.py:42
  298.8 3.6 collective-permute-done.23.other_ref
  305.1 4.2 %shard_map.235 = (bf16[512,1024]{1,0:T(8,128)(2,1)}, f32[8,1024]{1,0:T(8,128)S(1)}) custom-call(bf16[512,1024]{1,0:T(8,128)(2,1)S(1)} %copy-done.1, f32[512,1024]{1,0:T(8,128)S(1)} %fusion.37.own_ref, bf16[512,1024]{1,0:T(8,128)(2,1)} %collective-permute-done.23.other_ref, f32[512,1024]{1,0:T(8,128)S(1)} %copy-done.12, f32[6,1024]{1,0:T(8,128)S(1)} %copy-done.16), custom_call_target="tpu_custom_call" | custom-call | flops 10485760 | bytes 8388608 | tf_op jit(solution)/shard_map/pallas_call | solution.py:233
  313.2 3.8 fusion.7
  321.3 8.4 %collective-permute-done.30 = bf16[8,512]{1,0:T(8,128)(2,1)S(1)} collective-permute-done((bf16[8,512]{1,0:T(8,128)(2,1)S(1)}, bf16[8,512]{1,0:T(8,128)(2,1)S(1)}, u32[]{:S(2)}, u32[]{:S(2)}) %collective-permute-start.30) | collective-permute-done | bytes 8224 | tf_op jit(solution)/shard_map/ppermute | solution.py:260
  348.6 5.6 %collective-permute-done.34 = bf16[2,64,1024]{2,1,0:T(8,128)(2,1)S(1)} collective-permute-done((bf16[2,64,1024]{2,1,0:T(8,128)(2,1)S(1)}, bf16[2,64,1024]{2,1,0:T(8,128)(2,1)S(1)}, u32[]{:S(2)}, u32[]{:S(2)}) %collective-permute-start.34) | collective-permute-done | bytes 262176 | tf_op jit(solution)/shard_map/ppermute | solution.py:260
  354.2 3.7 collective-permute-done.35
  (341 shorter events, 161.6 us)
Async XLA Ops:
  7.2 66.2 %all-gather.3.cloned.1.call-start = ((), (), s32[]{:S(2)}) async-start(), calls=%async_computation.1 | async-start | bytes 5570560 | tf_op jit(solution)/shard_map/all_gather | solution.py:423
  7.3 5.5 %collective-permute-start.14 = (bf16[64,512]{1,0:T(8,128)(2,1)}, bf16[64,512]{1,0:T(8,128)(2,1)S(1)}, u32[]{:S(2)}, u32[]{:S(2)}) collective-permute-start(bf16[64,512]{1,0:T(8,128)(2,1)} %bitcast.228), channel_id=1, source_target_pairs={{0,1},{1,0},{2,3},{3,2},{4,5},{5,4},{6,7},{7,6},{8,9},{9,8},{10,11... | collective-permute-start | bytes 196616 | tf_op jit(solution)/shard_map/ppermute | solution.py:257
  14.4 135.4 %all-gather.5.cloned.1.call-start = ((), (), s32[]{:S(2)}) async-start(), calls=%async_computation.2 | async-start | bytes 8912896 | tf_op jit(solution)/shard_map/all_gather | solution.py:436
  25.1 6.3 %collective-permute-start.5 = (bf16[4,1536]{1,0:T(4,128)(2,1)S(1)}, bf16[4,1536]{1,0:T(4,128)(2,1)S(1)}, u32[]{:S(2)}, u32[]{:S(2)}) collective-permute-start(bf16[4,1536]{1,0:T(4,128)(2,1)S(1)} %pad_maximum_fusion.15), channel_id=1, source_target_pairs={{0,24},{2,26},{4,28},{6,30},{8,16},{10,18},{12,20},{14,22},{16,8},... | collective-permute-start | bytes 36872 | tf_op jit(solution)/shard_map/ppermute | solution.py:260
  34.5 283.7 %reduce-scatter.2.cloned.1.call-start = ((), (), s32[]{:S(2)}) async-start(), calls=%async_computation.3 | async-start | bytes 8912896 | tf_op jit(solution)/shard_map/reduce_scatter | solution.py:519
  34.5 27.2 %collective-permute-start.12 = (bf16[512,1024]{1,0:T(8,128)(2,1)}, bf16[512,1024]{1,0:T(8,128)(2,1)S(1)}, u32[]{:S(2)}, u32[]{:S(2)}) collective-permute-start(bf16[512,1024]{1,0:T(8,128)(2,1)} %tokens_ref.3), channel_id=1, source_target_pairs={{0,1},{1,0},{2,3},{3,2},{4,5},{5,4},{6,7},{7,6},{8,9},{9,8},{10,11... | collective-permute-start | bytes 3145736 | tf_op jit(solution)/shard_map/ppermute | solution.py:257
  42.2 8.2 %collective-permute-start.6 = (f32[4,6,512]{2,1,0:T(8,128)}, f32[4,6,512]{2,1,0:T(8,128)}, u32[]{:S(2)}, u32[]{:S(2)}) collective-permute-start(f32[4,6,512]{2,1,0:T(8,128)} %get-tuple-element.163), channel_id=1, source_target_pairs={{0,8},{2,10},{4,12},{6,14},{8,0},{10,2},{12,4},{14,6},{16,24},{18,... | collective-permute-start | bytes 147464 | tf_op jit(solution)/shard_map/ppermute | solution.py:260
  43.7 9.7 %collective-permute-start.7 = (f32[4,6,512]{2,1,0:T(8,128)}, f32[4,6,512]{2,1,0:T(8,128)}, u32[]{:S(2)}, u32[]{:S(2)}) collective-permute-start(f32[4,6,512]{2,1,0:T(8,128)} %get-tuple-element.164), channel_id=1, source_target_pairs={{0,16},{2,18},{4,20},{6,22},{8,24},{10,26},{12,28},{14,30},{16,0},... | collective-permute-start | bytes 147464 | tf_op jit(solution)/shard_map/ppermute | solution.py:260
  44.0 9.4 %collective-permute-start.8 = (f32[4,6,512]{2,1,0:T(8,128)}, f32[4,6,512]{2,1,0:T(8,128)}, u32[]{:S(2)}, u32[]{:S(2)}) collective-permute-start(f32[4,6,512]{2,1,0:T(8,128)} %get-tuple-element.165), channel_id=1, source_target_pairs={{0,24},{2,26},{4,28},{6,30},{8,16},{10,18},{12,20},{14,22},{16,8},... | collective-permute-start | bytes 147464 | tf_op jit(solution)/shard_map/ppermute | solution.py:260
  62.6 30.1 %collective-permute-start.15 = (bf16[512,1024]{1,0:T(8,128)(2,1)S(1)}, bf16[512,1024]{1,0:T(8,128)(2,1)}, u32[]{:S(2)}, u32[]{:S(2)}) collective-permute-start(bf16[512,1024]{1,0:T(8,128)(2,1)S(1)} %copy-done.2), channel_id=1, source_target_pairs={{0,1},{1,0},{2,3},{3,2},{4,5},{5,4},{6,7},{7,6},{8,9},{9,8},{10,11... | collective-permute-start | bytes 3145736 | tf_op jit(solution)/shard_map/ppermute | solution.py:257
  88.2 15.1 %collective-permute-start.16 = (bf16[512,512]{1,0:T(8,128)(2,1)S(1)}, bf16[512,512]{1,0:T(8,128)(2,1)S(1)}, u32[]{:S(2)}, u32[]{:S(2)}) collective-permute-start(bf16[512,512]{1,0:T(8,128)(2,1)S(1)} %shard_map.229), channel_id=1, source_target_pairs={{0,1},{1,0},{2,3},{3,2},{4,5},{5,4},{6,7},{7,6},{8,9},{9,8},{10,11... | collective-permute-start | bytes 1572872 | tf_op jit(solution)/shard_map/ppermute | solution.py:257
  111.6 25.3 %collective-permute-start.17 = (bf16[512,1024]{1,0:T(8,128)(2,1)}, bf16[512,1024]{1,0:T(8,128)(2,1)}, u32[]{:S(2)}, u32[]{:S(2)}) collective-permute-start(bf16[512,1024]{1,0:T(8,128)(2,1)} %get-tuple-element.64), channel_id=1, source_target_pairs={{0,1},{1,0},{2,3},{3,2},{4,5},{5,4},{6,7},{7,6},{8,9},{9,8},{10,11... | collective-permute-start | bytes 3145736 | tf_op jit(solution)/shard_map/ppermute | solution.py:257
  164.3 38.8 %collective-permute-start.18 = (bf16[512,1024]{1,0:T(8,128)(2,1)}, bf16[512,1024]{1,0:T(8,128)(2,1)}, u32[]{:S(2)}, u32[]{:S(2)}) collective-permute-start(bf16[512,1024]{1,0:T(8,128)(2,1)} %fusion.56), channel_id=1, source_target_pairs={{0,1},{1,0},{2,3},{3,2},{4,5},{5,4},{6,7},{7,6},{8,9},{9,8},{10,11... | collective-permute-start | bytes 3145736 | tf_op jit(solution)/shard_map/ppermute | solution.py:257
  210.4 13.8 %collective-permute-start.19 = (bf16[512,512]{1,0:T(8,128)(2,1)S(1)}, bf16[512,512]{1,0:T(8,128)(2,1)S(1)}, u32[]{:S(2)}, u32[]{:S(2)}) collective-permute-start(bf16[512,512]{1,0:T(8,128)(2,1)S(1)} %convolution_convert_fusion.3), channel_id=1, source_target_pairs={{0,1},{1,0},{2,3},{3,2},{4,5},{5,4},{6,7},{7,6},{8,9},{9,8},{10,11... | collective-permute-start | bytes 1572872 | tf_op jit(solution)/shard_map/ppermute | solution.py:257
  224.2 22.1 %collective-permute-start.21 = (f32[1024]{0:T(1024)S(1)}, f32[1024]{0:T(1024)S(1)}, u32[]{:S(2)}, u32[]{:S(2)}) collective-permute-start(f32[1024]{0:T(1024)S(1)} %bitcast.231), channel_id=1, source_target_pairs={{0,1},{1,0},{2,3},{3,2},{4,5},{5,4},{6,7},{7,6},{8,9},{9,8},{10,11... | collective-permute-start | bytes 12296 | tf_op jit(solution)/shard_map/ppermute | solution.py:257
  224.9 25.3 %collective-permute-start.20 = (bf16[1024,512]{1,0:T(8,128)(2,1)}, bf16[1024,512]{1,0:T(8,128)(2,1)}, u32[]{:S(2)}, u32[]{:S(2)}) collective-permute-start(bf16[1024,512]{1,0:T(8,128)(2,1)} %convolution_convert_fusion.2), channel_id=1, source_target_pairs={{0,1},{1,0},{2,3},{3,2},{4,5},{5,4},{6,7},{7,6},{8,9},{9,8},{10,11... | collective-permute-start | bytes 3145736 | tf_op jit(solution)/shard_map/ppermute | solution.py:257
  250.2 23.4 %collective-permute-start.22 = (bf16[512,1024]{1,0:T(8,128)(2,1)}, bf16[512,1024]{1,0:T(8,128)(2,1)S(1)}, u32[]{:S(2)}, u32[]{:S(2)}) collective-permute-start(bf16[512,1024]{1,0:T(8,128)(2,1)} %fusion.57), channel_id=1, source_target_pairs={{0,1},{1,0},{2,3},{3,2},{4,5},{5,4},{6,7},{7,6},{8,9},{9,8},{10,11... | collective-permute-start | bytes 3145736 | tf_op jit(solution)/shard_map/ppermute | solution.py:257
  278.6 23.8 %collective-permute-start.23 = (bf16[512,1024]{1,0:T(8,128)(2,1)}, bf16[512,1024]{1,0:T(8,128)(2,1)}, u32[]{:S(2)}, u32[]{:S(2)}) collective-permute-start(bf16[512,1024]{1,0:T(8,128)(2,1)} %fusion.51), channel_id=1, source_target_pairs={{0,1},{1,0},{2,3},{3,2},{4,5},{5,4},{6,7},{7,6},{8,9},{9,8},{10,11... | collective-permute-start | bytes 3145736 | tf_op jit(solution)/shard_map/ppermute | solution.py:257
  304.3 8.8 %collective-permute-start.24 = (bf16[2,2,2,64,2176]{4,3,0,1,2:T(8,128)(2,1)}, bf16[2,2,2,64,2176]{4,3,0,1,2:T(8,128)(2,1)}, u32[]{:S(2)}, u32[]{:S(2)}) collective-permute-start(bf16[2,2,2,64,2176]{4,3,0,1,2:T(8,128)(2,1)} %select_bitcast_fusion), channel_id=1, source_target_pairs={{0,2},{2,0},{4,6},{6,4},{8,10},{10,8},{12,14},{14,12},{16,18},{18,... | collective-permute-start | bytes 6684680 | tf_op jit(solution)/shard_map/ppermute | solution.py:260
  317.8 20.7 %collective-permute-start.25 = (bf16[2,2,64,1024]{3,2,0,1:T(8,128)(2,1)}, bf16[2,2,64,1024]{3,2,0,1:T(8,128)(2,1)S(1)}, u32[]{:S(2)}, u32[]{:S(2)}) collective-permute-start(bf16[2,2,64,1024]{3,2,0,1:T(8,128)(2,1)} %select_bitcast_fusion.1), channel_id=1, source_target_pairs={{0,4},{2,6},{4,0},{6,2},{8,12},{10,14},{12,8},{14,10},{16,20},{18,... | collective-permute-start | bytes 1572872 | tf_op jit(solution)/shard_map/ppermute | solution.py:260
  318.1 11.6 %collective-permute-start.30 = (bf16[8,512]{1,0:T(8,128)(2,1)S(1)}, bf16[8,512]{1,0:T(8,128)(2,1)S(1)}, u32[]{:S(2)}, u32[]{:S(2)}) collective-permute-start(bf16[8,512]{1,0:T(8,128)(2,1)S(1)} %pad_maximum_fusion.17), channel_id=1, source_target_pairs={{0,6},{2,4},{4,2},{6,0},{8,14},{10,12},{12,10},{14,8},{16,22},{18,... | collective-permute-start | bytes 24584 | tf_op jit(solution)/shard_map/ppermute | solution.py:260
  318.6 11.1 %collective-permute-start.29 = (bf16[8,512]{1,0:T(8,128)(2,1)S(1)}, bf16[8,512]{1,0:T(8,128)(2,1)S(1)}, u32[]{:S(2)}, u32[]{:S(2)}) collective-permute-start(bf16[8,512]{1,0:T(8,128)(2,1)S(1)} %pad_maximum_fusion.17), channel_id=1, source_target_pairs={{0,2},{2,0},{4,6},{6,4},{8,10},{10,8},{12,14},{14,12},{16,18},{18,... | collective-permute-start | bytes 24584 | tf_op jit(solution)/shard_map/ppermute | solution.py:260
  320.0 11.5 %collective-permute-start.28 = (bf16[8,512]{1,0:T(8,128)(2,1)S(1)}, bf16[8,512]{1,0:T(8,128)(2,1)S(1)}, u32[]{:S(2)}, u32[]{:S(2)}) collective-permute-start(bf16[8,512]{1,0:T(8,128)(2,1)S(1)} %pad_maximum_fusion.17), channel_id=1, source_target_pairs={{0,4},{2,6},{4,0},{6,2},{8,12},{10,14},{12,8},{14,10},{16,20},{18,... | collective-permute-start | bytes 24584 | tf_op jit(solution)/shard_map/ppermute | solution.py:260
  320.4 18.1 %collective-permute-start.26 = (bf16[2,2,64,1152]{3,2,0,1:T(8,128)(2,1)S(1)}, bf16[2,2,64,1152]{3,2,0,1:T(8,128)(2,1)S(1)}, u32[]{:S(2)}, u32[]{:S(2)}) collective-permute-start(bf16[2,2,64,1152]{3,2,0,1:T(8,128)(2,1)S(1)} %fusion.66), channel_id=1, source_target_pairs={{0,8},{2,10},{4,12},{6,14},{8,0},{10,2},{12,4},{14,6},{16,24},{18,... | collective-permute-start | bytes 1769480 | tf_op jit(solution)/shard_map/ppermute | solution.py:260
  331.6 6.6 %collective-permute-start.33 = (bf16[4,8,512]{2,1,0:T(8,128)(2,1)S(1)}, bf16[4,8,512]{2,1,0:T(8,128)(2,1)S(1)}, u32[]{:S(2)}, u32[]{:S(2)}) collective-permute-start(bf16[4,8,512]{2,1,0:T(8,128)(2,1)S(1)} %pad_maximum_fusion.13), channel_id=1, source_target_pairs={{0,24},{2,26},{4,28},{6,30},{8,16},{10,18},{12,20},{14,22},{16,8},... | collective-permute-start | bytes 98312 | tf_op jit(solution)/shard_map/ppermute | solution.py:260
  341.7 12.5 %collective-permute-start.34 = (bf16[2,64,1024]{2,1,0:T(8,128)(2,1)S(1)}, bf16[2,64,1024]{2,1,0:T(8,128)(2,1)S(1)}, u32[]{:S(2)}, u32[]{:S(2)}) collective-permute-start(bf16[2,64,1024]{2,1,0:T(8,128)(2,1)S(1)} %select_bitcast_fusion.2), channel_id=1, source_target_pairs={{0,8},{2,10},{4,12},{6,14},{8,0},{10,2},{12,4},{14,6},{16,24},{18,... | collective-permute-start | bytes 786440 | tf_op jit(solution)/shard_map/ppermute | solution.py:260
  343.3 14.6 %collective-permute-start.35 = (bf16[2,64,1152]{2,1,0:T(8,128)(2,1)S(1)}, bf16[2,64,1152]{2,1,0:T(8,128)(2,1)S(1)}, u32[]{:S(2)}, u32[]{:S(2)}) collective-permute-start(bf16[2,64,1152]{2,1,0:T(8,128)(2,1)S(1)} %fusion.73), channel_id=1, source_target_pairs={{0,16},{2,18},{4,20},{6,22},{8,24},{10,26},{12,28},{14,30},{16,0},... | collective-permute-start | bytes 884744 | tf_op jit(solution)/shard_map/ppermute | solution.py:260
  361.3 12.1 %collective-permute-start.43 = (bf16[64,1024]{1,0:T(8,128)(2,1)S(1)}, bf16[64,1024]{1,0:T(8,128)(2,1)S(1)}, u32[]{:S(2)}, u32[]{:S(2)}) collective-permute-start(bf16[64,1024]{1,0:T(8,128)(2,1)S(1)} %select_bitcast_fusion.4), channel_id=1, source_target_pairs={{0,16},{2,18},{4,20},{6,22},{8,24},{10,26},{12,28},{14,30},{16,0},... | collective-permute-start | bytes 393224 | tf_op jit(solution)/shard_map/ppermute | solution.py:260
  362.3 6.0 %collective-permute-start.42 = (f32[4,16,64]{2,1,0:T(8,128)S(1)}, f32[4,16,64]{2,1,0:T(8,128)S(1)}, u32[]{:S(2)}, u32[]{:S(2)}) collective-permute-start(f32[4,16,64]{2,1,0:T(8,128)S(1)} %pad_maximum_fusion.14), channel_id=1, source_target_pairs={{0,24},{2,26},{4,28},{6,30},{8,16},{10,18},{12,20},{14,22},{16,8},... | collective-permute-start | bytes 49160 | tf_op jit(solution)/shard_map/ppermute | solution.py:260
  364.7 6.1 %collective-permute-start.41 = (f32[4,16,64]{2,1,0:T(8,128)S(1)}, f32[4,16,64]{2,1,0:T(8,128)S(1)}, u32[]{:S(2)}, u32[]{:S(2)}) collective-permute-start(f32[4,16,64]{2,1,0:T(8,128)S(1)} %pad_maximum_fusion.14), channel_id=1, source_target_pairs={{0,8},{2,10},{4,12},{6,14},{8,0},{10,2},{12,4},{14,6},{16,24},{18,... | collective-permute-start | bytes 49160 | tf_op jit(solution)/shard_map/ppermute | solution.py:260
  365.0 7.7 %collective-permute-start.40 = (f32[4,16,64]{2,1,0:T(8,128)S(1)}, f32[4,16,64]{2,1,0:T(8,128)S(1)}, u32[]{:S(2)}, u32[]{:S(2)}) collective-permute-start(f32[4,16,64]{2,1,0:T(8,128)S(1)} %pad_maximum_fusion.14), channel_id=1, source_target_pairs={{0,16},{2,18},{4,20},{6,22},{8,24},{10,26},{12,28},{14,30},{16,0},... | collective-permute-start | bytes 49160 | tf_op jit(solution)/shard_map/ppermute | solution.py:260
  366.7 6.8 %collective-permute-start.44 = (bf16[64,1152]{1,0:T(8,128)(2,1)S(1)}, bf16[64,1152]{1,0:T(8,128)(2,1)S(1)}, u32[]{:S(2)}, u32[]{:S(2)}) collective-permute-start(bf16[64,1152]{1,0:T(8,128)(2,1)S(1)} %select_bitcast_fusion.3), channel_id=1, source_target_pairs={{0,4},{2,6},{4,0},{6,2},{8,12},{10,14},{12,8},{14,10},{16,20},{18,... | collective-permute-start | bytes 442376 | tf_op jit(solution)/shard_map/ppermute | solution.py:260
  (72 other events, 469.3 us)
Sparse Core Ops, SparseCore 0:
  14.5 58.9 all-gather.2
  76.2 73.5 all-gather.4
  197.8 102.0 reduce-scatter.1
where the time goes:
time: 391 us; the launch traced here: 383 us
  matrix products  85.7 us (22%)
  waiting for transfers between devices  79.6 us (20%)
  Pallas kernels  66.4 us (17%)
  starting transfers between devices  50 us (13%)
  other arithmetic  47.1 us (12%)
  local copies, waits for them, and re-layouts  39.3 us (10%)
  between operations  15.3 us (4%)
    pallas_call x2, Pallas kernels, attention_back(): pl.pallas_call(functools.partial(attend_back_kernel, head_size), out_shap...  36 us
    ppermute x31, waiting for transfers between devices, swap(): lax.ppermute(values, 'dp', [(i, i ^ mask) for i in range(self.dp_size)])  34.5 us
    dot_general x7, matrix products, dot_rows(): lax.dot_general(left, right, (((1,), (0,)), ((), ())), preferred_element_...  33.1 us
    ppermute x31, starting transfers between devices, swap(): lax.ppermute(values, 'dp', [(i, i ^ mask) for i in range(self.dp_size)])  32.1 us
    ppermute x14, waiting for transfers between devices, across(): return lax.ppermute(values, 'tensor', [(0, 1), (1, 0)])  31.6 us
    dot_general x8, matrix products, dot_last(): lax.dot_general(left, right, (((1,), (1,)), ((), ())), preferred_element_...  27.5 us
    ppermute x14, starting transfers between devices, across(): return lax.ppermute(values, 'tensor', [(0, 1), (1, 0)])  17.8 us
    unnamed x118, local copies, waits for them, and re-layouts  17.7 us
  transfers between devices with their start and end apart: 48, of which 24 were waited for; matrix products, arithmetic and copies ran while one was open for 36% of the time, Pallas kernels for 17%

commit v1 on v0

--- a/solution.py
+++ b/solution.py
@@ -132,7 +132,7 @@
             column_spec(rows, lanes, 2 * count),
         ],
         out_specs=column_spec(here, lanes, 0),
-        compiler_params=pltpu.CompilerParams(vmem_limit_bytes=40 * 1024 * 1024),
+        compiler_params=pltpu.CompilerParams(vmem_limit_bytes=60 * 1024 * 1024),
         cost_estimate=pl.CostEstimate(
             flops=16 * work,
             bytes_accessed=8 * rows * part_width,
@@ -166,7 +166,7 @@
         out_specs=pl.BlockSpec((rows, lanes), lambda j, p: (0, p * count + first + j)),
         scratch_shapes=[sums, sums],
         input_output_aliases=aliases,
-        compiler_params=pltpu.CompilerParams(vmem_limit_bytes=48 * 1024 * 1024),
+        compiler_params=pltpu.CompilerParams(vmem_limit_bytes=60 * 1024 * 1024),
         cost_estimate=pl.CostEstimate(
             flops=40 * work,
             bytes_accessed=14 * rows * blocks * lanes,
@@ -553,7 +553,9 @@
     def token_sum(values):
         return jnp.sum(values, axis=0, dtype=f32)
 
-    head_sums = token_sum(grad_hidden_all)
+    head_sums = sum(token_sum(v) for v in grad_hidden)
+    if paired:
+        head_sums, grad_attended = plan.hold(head_sums, grad_attended)
     head_sums = head_sums.reshape(-1, dp_size, piece).transpose(1, 0, 2).reshape(dp_size, -1)
     bias_sums = jnp.concatenate(
         [

time: 391 us -> 388 us (level)
  local copies, waits for them, and re-layouts: 39.3 us -> 30.9 us
  Pallas kernels: 66.4 us -> 72.3 us
    unnamed x118, local copies, waits for them, and re-layouts: 17.7 us -> 12.2 us
  transfers between devices with their start and end apart: 48 -> 48, of which waited for: 24 -> 27; matrix products, arithmetic and copies ran while one was open for 36% -> 36% of each run, Pallas kernels for 17% -> 19%
where the time goes in v1:
time: 388 us; the launch traced here: 381 us
  matrix products  88.2 us (23%)
  waiting for transfers between devices  78.4 us (20%)
  Pallas kernels  72.3 us (19%)
  starting transfers between devices  49.5 us (13%)
  other arithmetic  46.1 us (12%)
  local copies, waits for them, and re-layouts  30.9 us (8%)
  between operations  15.3 us (4%)
    pallas_call x2, Pallas kernels, attention_back(): pl.pallas_call(functools.partial(attend_back_kernel, head_size), out_shap...  39.3 us
    ppermute x31, waiting for transfers between devices, swap(): lax.ppermute(values, 'dp', [(i, i ^ mask) for i in range(self.dp_size)])  36.2 us
    dot_general x7, matrix products, dot_rows(): lax.dot_general(left, right, (((1,), (0,)), ((), ())), preferred_element_...  34.5 us
    ppermute x14, waiting for transfers between devices, across(): return lax.ppermute(values, 'tensor', [(0, 1), (1, 0)])  31.1 us
    ppermute x31, starting transfers between devices, swap(): lax.ppermute(values, 'dp', [(i, i ^ mask) for i in range(self.dp_size)])  31 us
    dot_general x8, matrix products, dot_last(): lax.dot_general(left, right, (((1,), (1,)), ((), ())), preferred_element_...  28.5 us
    pallas_call x2, Pallas kernels, attention(): pl.pallas_call(functools.partial(attend_kernel, head_size), out_shape=jax...  20 us
    ppermute x14, starting transfers between devices, across(): return lax.ppermute(values, 'tensor', [(0, 1), (1, 0)])  18.4 us
  transfers between devices with their start and end apart: 48, of which 27 were waited for; matrix products, arithmetic and copies ran while one was open for 36% of the time, Pallas kernels for 19%

profile of v1, /device:TPU:0, one launch (start us, length us, event | category | flops | bytes accessed | tf_op | source)
XLA Modules:
  0.0 380.7 jit_solution(17655063132279564373)
XLA Ops:
  7.3 3.0 collective-permute-start.14
  25.1 3.7 collective-permute-start.5
  50.3 4.1 %collective-permute-done.7 = f32[4,6,512]{2,1,0:T(8,128)} collective-permute-done((f32[4,6,512]{2,1,0:T(8,128)}, f32[4,6,512]{2,1,0:T(8,128)}, u32[]{:S(2)}, u32[]{:S(2)}) %collective-permute-start.7) | collective-permute-done | bytes 49184 | tf_op jit(solution)/shard_map/ppermute | solution.py:260
  70.3 3.4 all-gather.3.cloned.1.call-done
  73.7 7.7 %add_convert_fusion.q_ref.k_ref.v_ref = bf16[1024,1536]{1,0:T(8,128)(2,1)} fusion(f32[1536]{0:T(1024)} %pad_maximum_fusion.16, bf16[1024,2560]{1,0:T(8,128)(2,1)} %all-gather.3.cloned.1.call-done, bf16[512,1024]{1,0:T(8,128)(2,1)} %get-tuple-element.214, bf16[512,1024]{1,0:T(8,128)(2,1)} %get-tuple-element.213), kind=kOutput, calls=%fused_computation.4 | convolution fusion | flops 3228565504 | bytes 8396800 | tf_op jit(solution)/shard_map/dot_general | solution.py:34
  81.4 10.1 %shard_map.229 = bf16[512,512]{1,0:T(8,128)(2,1)} custom-call(bf16[1024,1536]{1,0:T(8,128)(2,1)} %add_convert_fusion.q_ref.k_ref.v_ref, bf16[1024,1536]{1,0:T(8,128)(2,1)} %add_convert_fusion.q_ref.k_ref.v_ref, bf16[1024,1536]{1,0:T(8,128)(2,1)} %add_convert_fusion.q_ref.k_ref.v_ref), custom_call_target="tpu_custom_call" | custom-call | flops 4294967296 | bytes 4194304 | tf_op jit(solution)/shard_map/pallas_call | solution.py:125
  94.5 9.9 %shard_map.228 = bf16[512,512]{1,0:T(8,128)(2,1)} custom-call(bf16[1024,1536]{1,0:T(8,128)(2,1)} %add_convert_fusion.q_ref.k_ref.v_ref, bf16[1024,1536]{1,0:T(8,128)(2,1)} %add_convert_fusion.q_ref.k_ref.v_ref, bf16[1024,1536]{1,0:T(8,128)(2,1)} %add_convert_fusion.q_ref.k_ref.v_ref), custom_call_target="tpu_custom_call" | custom-call | flops 4294967296 | bytes 4194304 | tf_op jit(solution)/shard_map/pallas_call | solution.py:125
  117.6 3.4 fusion.98
  124.1 15.2 %collective-permute-done.17 = bf16[512,1024]{1,0:T(8,128)(2,1)} collective-permute-done((bf16[512,1024]{1,0:T(8,128)(2,1)}, bf16[512,1024]{1,0:T(8,128)(2,1)}, u32[]{:S(2)}, u32[]{:S(2)}) %collective-permute-start.17) | collective-permute-done | bytes 1048608 | tf_op jit(solution)/shard_map/ppermute | solution.py:257
  139.3 3.0 maximum_bitcast_fusion.2
  142.3 7.7 %all-gather.5.cloned.1.call-done = bf16[2,1024,2048]{2,1,0:T(8,128)(2,1)} async-done(((bf16[2,64,2048]{2,1,0:T(8,128)(2,1)}), bf16[2,1024,2048]{2,1,0:T(8,128)(2,1)}) %all-gather.5.cloned.1.call-update) | async-done | bytes 8388624 | tf_op jit(solution)/shard_map/all_gather | solution.py:436
  150.0 5.0 %fusion.32 = f32[512,2048]{1,0:T(8,128)S(1)} fusion(bf16[512,1024]{1,0:T(8,128)(2,1)} %collective-permute-done.17, bf16[2,1024,2048]{2,1,0:T(8,128)(2,1)} %all-gather.5.cloned.1.call-done), kind=kOutput, calls=%fused_computation.46 | convolution fusion | flops 2147483648 | bytes 9437184 | tf_op jit(solution)/shard_map/dot_general | solution.py:34
  155.3 5.5 %convert_reduce_fusion = (f32[2048]{0:T(1024)}, bf16[512,2048]{1,0:T(8,128)(2,1)S(1)}) fusion(f32[512,2048]{1,0:T(8,128)S(1)} %fusion.32, f32[2048]{0:T(1024)S(1)} %copy-done.48, bf16[512,1024]{1,0:T(8,128)(2,1)S(1)} %copy-done.23, bf16[2,1024,2048]{2,1,0:T(8,128)(2,1)S(1)} %copy-done.51), kind=kOutput, calls=%fused_computation.35 | convolution fusion | flops 2171598848 | bytes 11550720 | tf_op jit(solution)/shard_map/dot_general | solution.py:34
  160.8 3.4 fusion.56
  165.7 5.9 %multiply_convert_fusion = (bf16[512,2048]{1,0:T(8,128)(2,1)S(1)}, bf16[512,2048]{1,0:T(8,128)(2,1)S(1)}, f32[512,2048]{1,0:T(8,128)S(1)}) fusion(f32[512,2048]{1,0:T(8,128)S(1)} %fusion.32, f32[2048]{0:T(1024)S(1)} %copy-done.48, bf16[512,1024]{1,0:T(8,128)(2,1)} %get-tuple-element.66, bf16[2,1024,2048]{2,1,0:T(8,128)(2,1)S(1)} %copy-done.51), kind=kOutput, calls=%fused_computation.34 | convolution fusion | flops 2168455168 | bytes 17833984 | tf_op jit(solution)/shard_map/dot_general | solution.py:34
  171.7 5.6 %convert_reduce_fusion.1 = (f32[2048]{0:T(1024)}, bf16[512,2048]{1,0:T(8,128)(2,1)S(1)}) fusion(f32[512,2048]{1,0:T(8,128)S(1)} %get-tuple-element.219, f32[2048]{0:T(1024)S(1)} %copy-done.48, bf16[512,1024]{1,0:T(8,128)(2,1)S(1)} %copy-done.22, bf16[2,1024,2048]{2,1,0:T(8,128)(2,1)S(1)} %copy-done.51), kind=kOutput, calls=%fused_computation.36 | convolution fusion | flops 2171598848 | bytes 11550720 | tf_op jit(solution)/shard_map/dot_general | solution.py:34
  180.3 13.1 %fusion.4 = bf16[2,1024,2048]{2,1,0:T(8,128)(2,1)} fusion(bf16[1,1024,2048]{2,1,0:T(8,128)(2,1)S(1)} %maximum_bitcast_fusion.1, bf16[1,1024,2048]{2,1,0:T(8,128)(2,1)S(1)} %maximum_bitcast_fusion, bf16[1,1024,1024]{2,1,0:T(8,128)(2,1)S(1)} %copy-done.24, bf16[1,1024,1024]{2,1,0:T(8,128)(2,1)} %maximum_bitcast_fusion.2), kind=kOutput, calls=%fused_computation.9 | convolution fusion | flops 8600420352 | bytes 20971520 | tf_op jit(solution)/shard_map/dot_general | solution.py:513
  193.5 5.4 %fusion.29.own_ref = f32[512,1024]{1,0:T(8,128)S(1)} fusion(bf16[512,2048]{1,0:T(8,128)(2,1)} %copy-done.29, bf16[2,1024,2048]{2,1,0:T(8,128)(2,1)} %all-gather.5.cloned.1.call-done), kind=kOutput, calls=%fused_computation.43 | convolution fusion | flops 2147483648 | bytes 8388608 | tf_op jit(solution)/shard_map/dot_general | solution.py:38
  199.0 4.4 %shard_map.231 = (f32[512,1024]{1,0:T(8,128)S(1)}, bf16[512,1024]{1,0:T(8,128)(2,1)S(1)}, f32[8,1024]{1,0:T(8,128)S(1)}) custom-call(f32[512,1024]{1,0:T(8,128)S(1)} %copy-done.6, f32[512,1024]{1,0:T(8,128)S(1)} %convolution_add_fusion.branch_ref, f32[512,1024]{1,0:T(8,128)S(1)} %fusion.29.own_ref, bf16[512,1024]{1,0:T(8,128)(2,1)} %collective-permute-done.18.other_ref, ...), custom_call_target="tpu_custom_call" | custom-call | flops 10485760 | bytes 8388608 | tf_op jit(solution)/shard_map/pallas_call | solution.py:233
  213.0 3.3 fusion.57
  216.3 3.8 collective-permute-done.19
  223.1 19.6 %shard_map.232.refs_0_ = bf16[1024,1536]{1,0:T(8,128)(2,1)} custom-call(bf16[1024,1536]{1,0:T(8,128)(2,1)} %add_convert_fusion.q_ref.k_ref.v_ref, bf16[1024,1536]{1,0:T(8,128)(2,1)} %add_convert_fusion.q_ref.k_ref.v_ref, bf16[1024,1536]{1,0:T(8,128)(2,1)} %add_convert_fusion.q_ref.k_ref.v_ref, bf16[1024,512]{1,0:T(8,128)(2,1)} %pad_maximum_fusion.4.g_ref), custom_call_target="tpu_custom_call" | custom-call | flops 10737418240 | bytes 3670016 | tf_op jit(solution)/shard_map/pallas_call | solution.py:161
  249.7 19.7 %shard_map.233 = bf16[1024,1536]{1,0:T(8,128)(2,1)} custom-call(bf16[1024,1536]{1,0:T(8,128)(2,1)} %add_convert_fusion.q_ref.k_ref.v_ref, bf16[1024,1536]{1,0:T(8,128)(2,1)} %add_convert_fusion.q_ref.k_ref.v_ref, bf16[1024,1536]{1,0:T(8,128)(2,1)} %add_convert_fusion.q_ref.k_ref.v_ref, ...), custom_call_target="tpu_custom_call", output_to_operand_aliasing={{}: (4, {})} | custom-call | flops 10737418240 | bytes 3670016 | tf_op jit(solution)/shard_map/pallas_call | solution.py:161
  271.4 5.3 %fusion.51 = bf16[512,1024]{1,0:T(8,128)(2,1)} fusion(bf16[1024,2560]{1,0:T(8,128)(2,1)} %all-gather.3.cloned.1.call-done, bf16[1024,1536]{1,0:T(8,128)(2,1)} %shard_map.233), kind=kOutput, calls=%fused_computation.77 | convolution fusion | flops 1611137024 | bytes 5767168 | tf_op jit(solution)/shard_map/dot_general | solution.py:38
  277.6 4.1 %fusion.37.own_ref = f32[512,1024]{1,0:T(8,128)S(1)} fusion(bf16[512,1536]{1,0:T(8,128)(2,1)S(1)} %slice.238, bf16[1024,2560]{1,0:T(8,128)(2,1)} %all-gather.3.cloned.1.call-done), kind=kOutput, calls=%fused_computation.55 | convolution fusion | flops 1610612736 | bytes 6815744 | tf_op jit(solution)/shard_map/dot_general | solution.py:38
  289.5 6.1 %convolution_convert_fusion = bf16[1024,1536]{1,0:T(8,128)(2,1)S(1)} fusion(bf16[1024,1536]{1,0:T(8,128)(2,1)} %shard_map.233, bf16[512,1024]{1,0:T(8,128)(2,1)} %get-tuple-element.214, bf16[512,1024]{1,0:T(8,128)(2,1)} %get-tuple-element.213), kind=kOutput, calls=%fused_computation.38 | convolution fusion | flops 3226992640 | bytes 8388608 | tf_op jit(solution)/shard_map/dot_general | solution.py:42
  296.1 3.5 collective-permute-done.23.other_ref
  302.3 4.2 %shard_map.235 = (bf16[512,1024]{1,0:T(8,128)(2,1)}, f32[8,1024]{1,0:T(8,128)S(1)}) custom-call(bf16[512,1024]{1,0:T(8,128)(2,1)S(1)} %copy-done.1, f32[512,1024]{1,0:T(8,128)S(1)} %fusion.37.own_ref, bf16[512,1024]{1,0:T(8,128)(2,1)} %collective-permute-done.23.other_ref, f32[512,1024]{1,0:T(8,128)S(1)} %copy-done.9, f32[6,1024]{1,0:T(8,128)S(1)} %copy-done.15), custom_call_target="tpu_custom_call" | custom-call | flops 10485760 | bytes 8388608 | tf_op jit(solution)/shard_map/pallas_call | solution.py:233
  310.4 3.8 fusion.7
  318.8 8.4 %collective-permute-done.30 = bf16[8,512]{1,0:T(8,128)(2,1)S(1)} collective-permute-done((bf16[8,512]{1,0:T(8,128)(2,1)S(1)}, bf16[8,512]{1,0:T(8,128)(2,1)S(1)}, u32[]{:S(2)}, u32[]{:S(2)}) %collective-permute-start.30) | collective-permute-done | bytes 8224 | tf_op jit(solution)/shard_map/ppermute | solution.py:260
  345.9 5.2 %collective-permute-done.34 = bf16[2,64,1024]{2,1,0:T(8,128)(2,1)S(1)} collective-permute-done((bf16[2,64,1024]{2,1,0:T(8,128)(2,1)S(1)}, bf16[2,64,1024]{2,1,0:T(8,128)(2,1)S(1)}, u32[]{:S(2)}, u32[]{:S(2)}) %collective-permute-start.34) | collective-permute-done | bytes 262176 | tf_op jit(solution)/shard_map/ppermute | solution.py:260
  351.1 4.3 %collective-permute-done.35 = bf16[2,64,1152]{2,1,0:T(8,128)(2,1)S(1)} collective-permute-done((bf16[2,64,1152]{2,1,0:T(8,128)(2,1)S(1)}, bf16[2,64,1152]{2,1,0:T(8,128)(2,1)S(1)}, u32[]{:S(2)}, u32[]{:S(2)}) %collective-permute-start.35) | collective-permute-done | bytes 294944 | tf_op jit(solution)/shard_map/ppermute | solution.py:260
  (341 shorter events, 154.3 us)
Async XLA Ops:
  7.2 66.5 %all-gather.3.cloned.1.call-start = ((), (), s32[]{:S(2)}) async-start(), calls=%async_computation.1 | async-start | bytes 5570560 | tf_op jit(solution)/shard_map/all_gather | solution.py:423
  14.4 135.6 %all-gather.5.cloned.1.call-start = ((), (), s32[]{:S(2)}) async-start(), calls=%async_computation.2 | async-start | bytes 8912896 | tf_op jit(solution)/shard_map/all_gather | solution.py:436
  25.1 6.3 %collective-permute-start.5 = (bf16[4,1536]{1,0:T(4,128)(2,1)S(1)}, bf16[4,1536]{1,0:T(4,128)(2,1)S(1)}, u32[]{:S(2)}, u32[]{:S(2)}) collective-permute-start(bf16[4,1536]{1,0:T(4,128)(2,1)S(1)} %pad_maximum_fusion.15), channel_id=1, source_target_pairs={{0,24},{2,26},{4,28},{6,30},{8,16},{10,18},{12,20},{14,22},{16,8},... | collective-permute-start | bytes 36872 | tf_op jit(solution)/shard_map/ppermute | solution.py:260
  34.5 281.6 %reduce-scatter.2.cloned.1.call-start = ((), (), s32[]{:S(2)}) async-start(), calls=%async_computation.3 | async-start | bytes 8912896 | tf_op jit(solution)/shard_map/reduce_scatter | solution.py:519
  34.5 27.8 %collective-permute-start.12 = (bf16[512,1024]{1,0:T(8,128)(2,1)}, bf16[512,1024]{1,0:T(8,128)(2,1)S(1)}, u32[]{:S(2)}, u32[]{:S(2)}) collective-permute-start(bf16[512,1024]{1,0:T(8,128)(2,1)} %tokens_ref.3), channel_id=1, source_target_pairs={{0,1},{1,0},{2,3},{3,2},{4,5},{5,4},{6,7},{7,6},{8,9},{9,8},{10,11... | collective-permute-start | bytes 3145736 | tf_op jit(solution)/shard_map/ppermute | solution.py:257
  42.2 8.2 %collective-permute-start.6 = (f32[4,6,512]{2,1,0:T(8,128)}, f32[4,6,512]{2,1,0:T(8,128)}, u32[]{:S(2)}, u32[]{:S(2)}) collective-permute-start(f32[4,6,512]{2,1,0:T(8,128)} %get-tuple-element.167), channel_id=1, source_target_pairs={{0,8},{2,10},{4,12},{6,14},{8,0},{10,2},{12,4},{14,6},{16,24},{18,... | collective-permute-start | bytes 147464 | tf_op jit(solution)/shard_map/ppermute | solution.py:260
  43.7 10.8 %collective-permute-start.7 = (f32[4,6,512]{2,1,0:T(8,128)}, f32[4,6,512]{2,1,0:T(8,128)}, u32[]{:S(2)}, u32[]{:S(2)}) collective-permute-start(f32[4,6,512]{2,1,0:T(8,128)} %get-tuple-element.168), channel_id=1, source_target_pairs={{0,16},{2,18},{4,20},{6,22},{8,24},{10,26},{12,28},{14,30},{16,0},... | collective-permute-start | bytes 147464 | tf_op jit(solution)/shard_map/ppermute | solution.py:260
  44.0 10.5 %collective-permute-start.8 = (f32[4,6,512]{2,1,0:T(8,128)}, f32[4,6,512]{2,1,0:T(8,128)}, u32[]{:S(2)}, u32[]{:S(2)}) collective-permute-start(f32[4,6,512]{2,1,0:T(8,128)} %get-tuple-element.169), channel_id=1, source_target_pairs={{0,24},{2,26},{4,28},{6,30},{8,16},{10,18},{12,20},{14,22},{16,8},... | collective-permute-start | bytes 147464 | tf_op jit(solution)/shard_map/ppermute | solution.py:260
  63.1 31.4 %collective-permute-start.15 = (bf16[512,1024]{1,0:T(8,128)(2,1)S(1)}, bf16[512,1024]{1,0:T(8,128)(2,1)}, u32[]{:S(2)}, u32[]{:S(2)}) collective-permute-start(bf16[512,1024]{1,0:T(8,128)(2,1)S(1)} %copy-done.2), channel_id=1, source_target_pairs={{0,1},{1,0},{2,3},{3,2},{4,5},{5,4},{6,7},{7,6},{8,9},{9,8},{10,11... | collective-permute-start | bytes 3145736 | tf_op jit(solution)/shard_map/ppermute | solution.py:257
  91.5 14.3 %collective-permute-start.16 = (bf16[512,512]{1,0:T(8,128)(2,1)}, bf16[512,512]{1,0:T(8,128)(2,1)S(1)}, u32[]{:S(2)}, u32[]{:S(2)}) collective-permute-start(bf16[512,512]{1,0:T(8,128)(2,1)} %shard_map.229), channel_id=1, source_target_pairs={{0,1},{1,0},{2,3},{3,2},{4,5},{5,4},{6,7},{7,6},{8,9},{9,8},{10,11... | collective-permute-start | bytes 1572872 | tf_op jit(solution)/shard_map/ppermute | solution.py:257
  114.7 24.6 %collective-permute-start.17 = (bf16[512,1024]{1,0:T(8,128)(2,1)}, bf16[512,1024]{1,0:T(8,128)(2,1)}, u32[]{:S(2)}, u32[]{:S(2)}) collective-permute-start(bf16[512,1024]{1,0:T(8,128)(2,1)} %get-tuple-element.66), channel_id=1, source_target_pairs={{0,1},{1,0},{2,3},{3,2},{4,5},{5,4},{6,7},{7,6},{8,9},{9,8},{10,11... | collective-permute-start | bytes 3145736 | tf_op jit(solution)/shard_map/ppermute | solution.py:257
  164.3 34.7 %collective-permute-start.18 = (bf16[512,1024]{1,0:T(8,128)(2,1)}, bf16[512,1024]{1,0:T(8,128)(2,1)}, u32[]{:S(2)}, u32[]{:S(2)}) collective-permute-start(bf16[512,1024]{1,0:T(8,128)(2,1)} %fusion.56), channel_id=1, source_target_pairs={{0,1},{1,0},{2,3},{3,2},{4,5},{5,4},{6,7},{7,6},{8,9},{9,8},{10,11... | collective-permute-start | bytes 3145736 | tf_op jit(solution)/shard_map/ppermute | solution.py:257
  206.3 13.8 %collective-permute-start.19 = (bf16[512,512]{1,0:T(8,128)(2,1)S(1)}, bf16[512,512]{1,0:T(8,128)(2,1)S(1)}, u32[]{:S(2)}, u32[]{:S(2)}) collective-permute-start(bf16[512,512]{1,0:T(8,128)(2,1)S(1)} %convolution_convert_fusion.3), channel_id=1, source_target_pairs={{0,1},{1,0},{2,3},{3,2},{4,5},{5,4},{6,7},{7,6},{8,9},{9,8},{10,11... | collective-permute-start | bytes 1572872 | tf_op jit(solution)/shard_map/ppermute | solution.py:257
  220.1 23.3 %collective-permute-start.21 = (f32[1024]{0:T(1024)}, f32[1024]{0:T(1024)S(1)}, u32[]{:S(2)}, u32[]{:S(2)}) collective-permute-start(f32[1024]{0:T(1024)} %bitcast.23), channel_id=1, source_target_pairs={{0,1},{1,0},{2,3},{3,2},{4,5},{5,4},{6,7},{7,6},{8,9},{9,8},{10,11... | collective-permute-start | bytes 12296 | tf_op jit(solution)/shard_map/ppermute | solution.py:257
  221.8 24.4 %collective-permute-start.20 = (bf16[1024,512]{1,0:T(8,128)(2,1)}, bf16[1024,512]{1,0:T(8,128)(2,1)}, u32[]{:S(2)}, u32[]{:S(2)}) collective-permute-start(bf16[1024,512]{1,0:T(8,128)(2,1)} %convolution_convert_fusion.2), channel_id=1, source_target_pairs={{0,1},{1,0},{2,3},{3,2},{4,5},{5,4},{6,7},{7,6},{8,9},{9,8},{10,11... | collective-permute-start | bytes 3145736 | tf_op jit(solution)/shard_map/ppermute | solution.py:257
  246.2 23.3 %collective-permute-start.22 = (bf16[512,1024]{1,0:T(8,128)(2,1)}, bf16[512,1024]{1,0:T(8,128)(2,1)S(1)}, u32[]{:S(2)}, u32[]{:S(2)}) collective-permute-start(bf16[512,1024]{1,0:T(8,128)(2,1)} %fusion.57), channel_id=1, source_target_pairs={{0,1},{1,0},{2,3},{3,2},{4,5},{5,4},{6,7},{7,6},{8,9},{9,8},{10,11... | collective-permute-start | bytes 3145736 | tf_op jit(solution)/shard_map/ppermute | solution.py:257
  276.7 22.9 %collective-permute-start.23 = (bf16[512,1024]{1,0:T(8,128)(2,1)}, bf16[512,1024]{1,0:T(8,128)(2,1)}, u32[]{:S(2)}, u32[]{:S(2)}) collective-permute-start(bf16[512,1024]{1,0:T(8,128)(2,1)} %fusion.51), channel_id=1, source_target_pairs={{0,1},{1,0},{2,3},{3,2},{4,5},{5,4},{6,7},{7,6},{8,9},{9,8},{10,11... | collective-permute-start | bytes 3145736 | tf_op jit(solution)/shard_map/ppermute | solution.py:257
  301.5 8.8 %collective-permute-start.24 = (bf16[2,2,2,64,2176]{4,3,0,1,2:T(8,128)(2,1)}, bf16[2,2,2,64,2176]{4,3,0,1,2:T(8,128)(2,1)}, u32[]{:S(2)}, u32[]{:S(2)}) collective-permute-start(bf16[2,2,2,64,2176]{4,3,0,1,2:T(8,128)(2,1)} %select_bitcast_fusion), channel_id=1, source_target_pairs={{0,2},{2,0},{4,6},{6,4},{8,10},{10,8},{12,14},{14,12},{16,18},{18,... | collective-permute-start | bytes 6684680 | tf_op jit(solution)/shard_map/ppermute | solution.py:260
  315.0 21.8 %collective-permute-start.25 = (bf16[2,2,64,1024]{3,2,0,1:T(8,128)(2,1)}, bf16[2,2,64,1024]{3,2,0,1:T(8,128)(2,1)S(1)}, u32[]{:S(2)}, u32[]{:S(2)}) collective-permute-start(bf16[2,2,64,1024]{3,2,0,1:T(8,128)(2,1)} %select_bitcast_fusion.1), channel_id=1, source_target_pairs={{0,4},{2,6},{4,0},{6,2},{8,12},{10,14},{12,8},{14,10},{16,20},{18,... | collective-permute-start | bytes 1572872 | tf_op jit(solution)/shard_map/ppermute | solution.py:260
  316.1 11.2 %collective-permute-start.30 = (bf16[8,512]{1,0:T(8,128)(2,1)S(1)}, bf16[8,512]{1,0:T(8,128)(2,1)S(1)}, u32[]{:S(2)}, u32[]{:S(2)}) collective-permute-start(bf16[8,512]{1,0:T(8,128)(2,1)S(1)} %pad_maximum_fusion.17), channel_id=1, source_target_pairs={{0,6},{2,4},{4,2},{6,0},{8,14},{10,12},{12,10},{14,8},{16,22},{18,... | collective-permute-start | bytes 24584 | tf_op jit(solution)/shard_map/ppermute | solution.py:260
  316.1 11.1 %collective-permute-start.29 = (bf16[8,512]{1,0:T(8,128)(2,1)S(1)}, bf16[8,512]{1,0:T(8,128)(2,1)S(1)}, u32[]{:S(2)}, u32[]{:S(2)}) collective-permute-start(bf16[8,512]{1,0:T(8,128)(2,1)S(1)} %pad_maximum_fusion.17), channel_id=1, source_target_pairs={{0,2},{2,0},{4,6},{6,4},{8,10},{10,8},{12,14},{14,12},{16,18},{18,... | collective-permute-start | bytes 24584 | tf_op jit(solution)/shard_map/ppermute | solution.py:260
  317.3 11.5 %collective-permute-start.28 = (bf16[8,512]{1,0:T(8,128)(2,1)S(1)}, bf16[8,512]{1,0:T(8,128)(2,1)S(1)}, u32[]{:S(2)}, u32[]{:S(2)}) collective-permute-start(bf16[8,512]{1,0:T(8,128)(2,1)S(1)} %pad_maximum_fusion.17), channel_id=1, source_target_pairs={{0,4},{2,6},{4,0},{6,2},{8,12},{10,14},{12,8},{14,10},{16,20},{18,... | collective-permute-start | bytes 24584 | tf_op jit(solution)/shard_map/ppermute | solution.py:260
  318.3 18.5 %collective-permute-start.26 = (bf16[2,2,64,1152]{3,2,0,1:T(8,128)(2,1)S(1)}, bf16[2,2,64,1152]{3,2,0,1:T(8,128)(2,1)S(1)}, u32[]{:S(2)}, u32[]{:S(2)}) collective-permute-start(bf16[2,2,64,1152]{3,2,0,1:T(8,128)(2,1)S(1)} %fusion.66), channel_id=1, source_target_pairs={{0,8},{2,10},{4,12},{6,14},{8,0},{10,2},{12,4},{14,6},{16,24},{18,... | collective-permute-start | bytes 1769480 | tf_op jit(solution)/shard_map/ppermute | solution.py:260
  328.8 6.9 %collective-permute-start.33 = (bf16[4,8,512]{2,1,0:T(8,128)(2,1)S(1)}, bf16[4,8,512]{2,1,0:T(8,128)(2,1)S(1)}, u32[]{:S(2)}, u32[]{:S(2)}) collective-permute-start(bf16[4,8,512]{2,1,0:T(8,128)(2,1)S(1)} %pad_maximum_fusion.13), channel_id=1, source_target_pairs={{0,24},{2,26},{4,28},{6,30},{8,16},{10,18},{12,20},{14,22},{16,8},... | collective-permute-start | bytes 98312 | tf_op jit(solution)/shard_map/ppermute | solution.py:260
  330.2 5.5 %collective-permute-start.32 = (bf16[4,8,512]{2,1,0:T(8,128)(2,1)S(1)}, bf16[4,8,512]{2,1,0:T(8,128)(2,1)S(1)}, u32[]{:S(2)}, u32[]{:S(2)}) collective-permute-start(bf16[4,8,512]{2,1,0:T(8,128)(2,1)S(1)} %pad_maximum_fusion.13), channel_id=1, source_target_pairs={{0,8},{2,10},{4,12},{6,14},{8,0},{10,2},{12,4},{14,6},{16,24},{18,... | collective-permute-start | bytes 98312 | tf_op jit(solution)/shard_map/ppermute | solution.py:260
  340.0 11.1 %collective-permute-start.34 = (bf16[2,64,1024]{2,1,0:T(8,128)(2,1)S(1)}, bf16[2,64,1024]{2,1,0:T(8,128)(2,1)S(1)}, u32[]{:S(2)}, u32[]{:S(2)}) collective-permute-start(bf16[2,64,1024]{2,1,0:T(8,128)(2,1)S(1)} %select_bitcast_fusion.2), channel_id=1, source_target_pairs={{0,8},{2,10},{4,12},{6,14},{8,0},{10,2},{12,4},{14,6},{16,24},{18,... | collective-permute-start | bytes 786440 | tf_op jit(solution)/shard_map/ppermute | solution.py:260
  340.6 14.8 %collective-permute-start.35 = (bf16[2,64,1152]{2,1,0:T(8,128)(2,1)S(1)}, bf16[2,64,1152]{2,1,0:T(8,128)(2,1)S(1)}, u32[]{:S(2)}, u32[]{:S(2)}) collective-permute-start(bf16[2,64,1152]{2,1,0:T(8,128)(2,1)S(1)} %fusion.73), channel_id=1, source_target_pairs={{0,16},{2,18},{4,20},{6,22},{8,24},{10,26},{12,28},{14,30},{16,0},... | collective-permute-start | bytes 884744 | tf_op jit(solution)/shard_map/ppermute | solution.py:260
  358.9 11.9 %collective-permute-start.43 = (bf16[64,1024]{1,0:T(8,128)(2,1)S(1)}, bf16[64,1024]{1,0:T(8,128)(2,1)S(1)}, u32[]{:S(2)}, u32[]{:S(2)}) collective-permute-start(bf16[64,1024]{1,0:T(8,128)(2,1)S(1)} %select_bitcast_fusion.4), channel_id=1, source_target_pairs={{0,16},{2,18},{4,20},{6,22},{8,24},{10,26},{12,28},{14,30},{16,0},... | collective-permute-start | bytes 393224 | tf_op jit(solution)/shard_map/ppermute | solution.py:260
  360.3 6.1 %collective-permute-start.42 = (f32[4,16,64]{2,1,0:T(8,128)S(1)}, f32[4,16,64]{2,1,0:T(8,128)S(1)}, u32[]{:S(2)}, u32[]{:S(2)}) collective-permute-start(f32[4,16,64]{2,1,0:T(8,128)S(1)} %pad_maximum_fusion.14), channel_id=1, source_target_pairs={{0,24},{2,26},{4,28},{6,30},{8,16},{10,18},{12,20},{14,22},{16,8},... | collective-permute-start | bytes 49160 | tf_op jit(solution)/shard_map/ppermute | solution.py:260
  362.6 5.6 %collective-permute-start.41 = (f32[4,16,64]{2,1,0:T(8,128)S(1)}, f32[4,16,64]{2,1,0:T(8,128)S(1)}, u32[]{:S(2)}, u32[]{:S(2)}) collective-permute-start(f32[4,16,64]{2,1,0:T(8,128)S(1)} %pad_maximum_fusion.14), channel_id=1, source_target_pairs={{0,8},{2,10},{4,12},{6,14},{8,0},{10,2},{12,4},{14,6},{16,24},{18,... | collective-permute-start | bytes 49160 | tf_op jit(solution)/shard_map/ppermute | solution.py:260
  362.6 7.4 %collective-permute-start.40 = (f32[4,16,64]{2,1,0:T(8,128)S(1)}, f32[4,16,64]{2,1,0:T(8,128)S(1)}, u32[]{:S(2)}, u32[]{:S(2)}) collective-permute-start(f32[4,16,64]{2,1,0:T(8,128)S(1)} %pad_maximum_fusion.14), channel_id=1, source_target_pairs={{0,16},{2,18},{4,20},{6,22},{8,24},{10,26},{12,28},{14,30},{16,0},... | collective-permute-start | bytes 49160 | tf_op jit(solution)/shard_map/ppermute | solution.py:260
  364.8 6.0 %collective-permute-start.44 = (bf16[64,1152]{1,0:T(8,128)(2,1)S(1)}, bf16[64,1152]{1,0:T(8,128)(2,1)S(1)}, u32[]{:S(2)}, u32[]{:S(2)}) collective-permute-start(bf16[64,1152]{1,0:T(8,128)(2,1)S(1)} %select_bitcast_fusion.3), channel_id=1, source_target_pairs={{0,4},{2,6},{4,0},{6,2},{8,12},{10,14},{12,8},{14,10},{16,20},{18,... | collective-permute-start | bytes 442376 | tf_op jit(solution)/shard_map/ppermute | solution.py:260
  (72 other events, 495.3 us)
Sparse Core Ops, SparseCore 0:
  14.5 59.1 all-gather.2
  76.4 73.4 all-gather.4
  193.5 101.9 reduce-scatter.1
